TPU v7x, 128 devices: a whole 4x4x4 slice. The times are simulated.
128 devices in a mesh: side: 2 (over core), grp: 4 (over y), dev: 16 (over x, z).
Axes of the slice: x: 4, y: 4, z: 4, core: 2. Of those that a mesh axis runs over, the one named last changes fastest.
Arguments:
- embeds: bfloat16 [2, 256, 256, 256], P('side', ('grp', 'dev')), may hold values from -16 to 16
- partners: int32 [256, 32], replicated, may hold values from 0 to 255, as said below
- counts: int32 [256], replicated, may hold values from 1 to 32, as said below
Outputs:
- mapped: bfloat16 [64, 2, 2, 256, 256], P(('grp', 'dev'), 'side')
- scale_b: float32 [256, 256], P(('grp', 'dev'))
Inputs may be any that keep to these rules, and one draw needn't show every extreme that they name: `partners`: entry t of row a is a B block id; only the first counts[a] entries of a row are candidates. The entries of one row lie on distinct devices of catalog B (distinct entry // 4). All entries of the rows of one device's A blocks that lie on the same device of catalog B name the same block. `counts`: some A block has 32 candidates.
All inputs are finite; a program needn't handle non-finite values.
Results may differ from a plain program's by a relative error of at most 0.015.
Values may be sent and summed in bfloat16 or wider, within the bound.
A program may use at most 128 MiB of HBM per device.

v0:
```python
import functools
import math

import jax
import jax.numpy as jnp
from jax import lax
from jax.experimental import pallas as pl
from jax.experimental.pallas import tpu as pltpu
from jax.sharding import PartitionSpec as P

ITERS = 3
GAIN = 20.0 * math.log2(math.e)
MESH = pl.DeviceIdType.MESH
NT = (((1,), (1,)), ((), ()))
f32 = jnp.float32
bf16 = jnp.bfloat16
PIECES = ((0, 96), (96, 80), (176, 80))


def place():
    d = lax.axis_index("dev")
    return lax.axis_index("side"), (d // 4, lax.axis_index("grp"), d % 4)


def flip_a(p):
    return p + 1 - 2 * (p % 2)


def flip_b(p):
    return 3 - p


def member(at, flip, bits, core):
    x, y, z = [flip(p) if (bits >> k) & 1 else p for k, p in enumerate(at)]
    return (core, y, x * 4 + z)


def dot(a, b):
    return jnp.dot(a, b, preferred_element_type=f32)


def dot_nt(a, b):
    return lax.dot_general(a, b, NT, preferred_element_type=f32)


def split_dot(onehot, values):
    high = values.astype(bf16)
    low = (values - high.astype(f32)).astype(bf16)
    return dot(onehot, high) + dot(onehot, low)


def kernel(
    T,
    idx,
    shift,
    x_ref,
    oa,
    oat,
    ob,
    obt,
    obd,
    mapped_ref,
    scale_ref,
    abuf,
    bbuf,
    tiles,
    row_norm,
    col_norm,
    sums,
    spread,
    dense,
    row_send,
    col_send,
    row_recv,
    col_recv,
    numer,
    ship,
    landed,
    own_sem,
    sib_sem,
    gather_sem,
    relay_sem,
    out_sem,
    row_sem,
    col_sem,
    half_sem,
):
    core, at = place()
    other = 1 - core
    sibling = member(at, flip_a, 0, other)
    flips = (flip_a, flip_b)
    bufs = (abuf, bbuf)

    barrier = pltpu.get_barrier_semaphore()
    greeted = [sibling]
    for m in range(1, 8):
        greeted += [member(at, flip_a, m, core), member(at, flip_b, m, core), member(at, flip_b, m, other)]
    for peer in greeted:
        pl.semaphore_signal(barrier, inc=1, device_id=peer, device_id_type=MESH)
    pl.semaphore_wait(barrier, len(greeted))

    def remote(src, dst, send, recv, peer):
        return pltpu.make_async_remote_copy(
            src_ref=src, dst_ref=dst, send_sem=send, recv_sem=recv, device_id=peer, device_id_type=MESH
        )

    @pl.when(core == 0)
    def _():
        give = remote(x_ref.at[pl.ds(2, 2)], abuf.at[pl.ds(0, 2)], sib_sem.at[0], sib_sem.at[1], sibling)
        give.start()
        mine = pltpu.make_async_copy(x_ref.at[pl.ds(0, 2)], abuf.at[pl.ds(0, 2)], own_sem.at[0])
        mine.start()
        mine.wait()
        give.wait_send()
        here = bbuf.at[pl.ds(0, 4)]
        pltpu.make_async_copy(here, here, sib_sem.at[1]).wait()

    @pl.when(core == 1)
    def _():
        give = remote(x_ref, bbuf.at[pl.ds(0, 4)], sib_sem.at[0], sib_sem.at[1], sibling)
        give.start()
        mine = pltpu.make_async_copy(x_ref, bbuf.at[pl.ds(0, 4)], own_sem.at[0])
        mine.start()
        mine.wait()
        give.wait_send()
        here = abuf.at[pl.ds(0, 2)]
        pltpu.make_async_copy(here, here, sib_sem.at[1]).wait()

    def unit(cat, slot, piece):
        start, size = PIECES[piece]
        if cat == 0:
            return abuf.at[pl.ds(slot * 2, 2), pl.ds(start, size)]
        return bbuf.at[pl.ds(slot * 4 + core * 2, 2), pl.ds(start, size)]

    def send_unit(cat, dim, piece, slot):
        there = slot ^ (1 << dim)
        copy = remote(
            unit(cat, slot, piece),
            unit(cat, there, piece),
            out_sem.at[0],
            gather_sem.at[cat, piece, there],
            member(at, flips[cat], 1 << dim, core),
        )
        copy.start()
        return copy

    sent = []
    relays = []

    def arrived(cat, piece, slot):
        here = unit(cat, slot, piece)
        pltpu.make_async_copy(here, here, gather_sem.at[cat, piece, slot]).wait()
        if cat == 1:
            copy = remote(here, here, out_sem.at[1], relay_sem.at[0], sibling)
            copy.start()
            relays.append(copy)

    for step in range(3):
        for dim in range(3):
            for cat in range(2):
                sent.append(send_unit(cat, dim, (dim - step) % 3, 0))

    def a_norms(slot):
        def body(i, c):
            x = abuf[slot * 2 + i].astype(f32)
            total = jnp.sum(x * x, axis=1, keepdims=True)
            row_norm[slot * 2 + i] = lax.rsqrt(total * (1.0 / 256.0) + 1e-06) * (GAIN / 16.0)
            return c

        lax.fori_loop(0, 2, body, 0)

    ones = jnp.ones((8, 256), bf16)

    def b_norms(slot):
        def body(i, c):
            y = bbuf[slot * 4 + i].astype(f32)
            y2 = y * y
            high = y2.astype(bf16)
            low = (y2 - high.astype(f32)).astype(bf16)
            total = dot_nt(ones, high) + dot_nt(ones, low)
            col_norm[slot * 4 + i] = lax.rsqrt(total * (1.0 / 256.0) + 1e-06) * (1.0 / 16.0)
            return c

        lax.fori_loop(0, 4, body, 0)

    a_norms(0)
    b_norms(0)
    for r in range(3):
        for cat in range(2):
            arrived(cat, r, 1 << r)
            sent.append(send_unit(cat, (r + 1) % 3, r, 1 << r))
    for r in range(3):
        for cat in range(2):
            sent.append(send_unit(cat, (r + 2) % 3, r, 1 << r))
    for r in range(3):
        for cat in range(2):
            near = 1 << ((r + 1) % 3)
            arrived(cat, r, near)
            sent.append(send_unit(cat, (r + 2) % 3, r, near))
    for r in range(3):
        for cat in range(2):
            far = (1 << ((r + 1) % 3)) | (1 << r)
            arrived(cat, r, far)
            sent.append(send_unit(cat, (r + 2) % 3, r, far))
    for r in range(3):
        last = 1 << ((r + 2) % 3)
        for rest in (0, 1 << r, 1 << ((r + 1) % 3), (1 << r) | (1 << ((r + 1) % 3))):
            for cat in range(2):
                arrived(cat, r, last | rest)
    for slot in range(1, 8):
        a_norms(slot)
    from_sibling = bbuf.at[pl.ds(4, 14)]
    pltpu.make_async_copy(from_sibling, from_sibling, relay_sem.at[0]).wait()
    for copy in sent:
        copy.wait_send()
    for copy in relays:
        copy.wait_send()
    for slot in range(1, 8):
        b_norms(slot)

    row_id = lax.broadcasted_iota(jnp.int32, (8, 256), 0)

    def build(i, c):
        total = jnp.zeros((8, 256), f32)
        for u in range(8):
            t = i * 8 + u
            a, b = idx[t], idx[T + t]
            scores = dot_nt(abuf[a], bbuf[b])
            tile = jnp.exp2(scores * row_norm[a] * col_norm[b][0:1] - shift[t]).astype(bf16)
            tiles[t] = tile
            total = jnp.where(row_id == u, dot_nt(ones, tile), total)
        sums[pl.ds(pl.multiple_of(i * 8, 8), 8), :] = total
        return c

    lax.fori_loop(0, T // 8, build, 0)

    def sweep(transposed):
        def body(i, c):
            rows = pl.ds(pl.multiple_of(i * 8, 8), 8)
            left = spread[rows, :].astype(bf16)
            total = jnp.zeros((8, 256), f32)
            for u in range(8):
                tile = tiles[i * 8 + u]
                part = dot_nt(left, tile) if transposed else dot(left, tile)
                total = jnp.where(row_id == u, part, total)
            sums[rows, :] = total
            return c

        lax.fori_loop(0, T // 8, body, 0)

    def row_exchange(phase):
        row_send[phase] = split_dot(oa[...], sums[...]).astype(bf16)
        copies = []
        for m in range(1, 8):
            copy = remote(
                row_send.at[phase], row_recv.at[phase, m], row_sem.at[0, phase], row_sem.at[1, phase],
                member(at, flip_a, m, core),
            )
            copy.start()
            copies.append(copy)
        return copies

    def row_result(phase, copies):
        got = row_recv.at[phase, pl.ds(1, 7)]
        pltpu.make_async_copy(got, got, row_sem.at[1, phase]).wait()
        total = row_send[phase].astype(f32)
        for m in range(1, 8):
            total += row_recv[phase, m].astype(f32)
        for copy in copies:
            copy.wait_send()
        return total

    def col_exchange(phase):
        col_send[phase] = split_dot(ob[...], sums[...]).astype(bf16)
        copies = []
        for far in range(2):
            for m in range(8):
                if far + m:
                    copy = remote(
                        col_send.at[phase], col_recv.at[phase, far * 8 + m], col_sem.at[0, phase],
                        col_sem.at[1, phase], member(at, flip_b, m, other if far else core),
                    )
                    copy.start()
                    copies.append(copy)
        got = col_recv.at[phase, pl.ds(1, 15)]
        pltpu.make_async_copy(got, got, col_sem.at[1, phase]).wait()
        total = col_send[phase].astype(f32)
        for m in range(1, 16):
            total += col_recv[phase, m].astype(f32)
        for copy in copies:
            copy.wait_send()
        return total

    for phase in range(ITERS):
        if phase:
            sweep(True)
        scale_a = 1.0 / row_result(phase, row_exchange(phase))
        spread[...] = dot(oat[...], scale_a.astype(bf16))
        sweep(False)
        scale_b = 1.0 / (1.0 + col_exchange(phase))
        spread[...] = dot(obt[...], scale_b.astype(bf16))
    x, y, z = at
    own_b = x // 2 + 2 * (y // 2) + 4 * (z // 2)
    sums[pl.ds(0, 32), :] = scale_b
    near_rows = sums[pl.ds(pl.multiple_of((own_b // 2) * 8, 8), 8), :]
    scale_ref[...] = jnp.where(own_b % 2 == 0, near_rows[0:4], near_rows[4:8])
    dense[...] = dot(obd[...], scale_b.astype(bf16))

    def partial(slot):
        def body(i, c):
            total = None
            base = (slot * 2 + i) * 8
            rows = dense[pl.ds(pl.multiple_of(base, 8), 8), :]
            for d in range(8):
                scaled = (tiles[idx[2 * T + base + d]] * rows[d : d + 1]).astype(bf16)
                part = dot(scaled, bbuf[idx[2 * T + 128 + base + d]])
                total = part if total is None else total + part
            numer[slot * 2 + i] = total
            return c

        lax.fori_loop(0, 2, body, 0)

    halves = []

    def send_half(piece, slot, dim, order):
        start, size = PIECES[piece]
        two, rows = pl.ds(slot * 2, 2), pl.ds(start, size)
        ship[two, rows, :] = numer[two, rows, :].astype(bf16)
        there = slot ^ (1 << dim)
        copy = remote(
            ship.at[two, rows], landed.at[order, pl.ds(there * 2, 2), rows], out_sem.at[2], half_sem.at[order, piece, there],
            member(at, flip_a, 1 << dim, core),
        )
        copy.start()
        halves.append(copy)

    def add_half(piece, slot, order):
        start, size = PIECES[piece]
        two, rows = pl.ds(slot * 2, 2), pl.ds(start, size)
        here = landed.at[order, two, rows]
        pltpu.make_async_copy(here, here, half_sem.at[order, piece, slot]).wait()
        numer[two, rows, :] = numer[two, rows, :] + landed[order, two, rows, :].astype(f32)

    for slot in (7, 3, 5, 6, 1, 2, 4, 0):
        partial(slot)
        for r in range(3):
            if (slot >> r) & 1:
                send_half(r, slot, r, 0)
    for r in range(3):
        k1, k2 = 1 << ((r + 1) % 3), 1 << ((r + 2) % 3)
        add_half(r, k1 | k2, 0)
        send_half(r, k1 | k2, (r + 1) % 3, 1)
    sweep(True)
    row_copies = row_exchange(ITERS)
    for r in range(3):
        k1, k2 = 1 << ((r + 1) % 3), 1 << ((r + 2) % 3)
        add_half(r, k1, 0)
        send_half(r, k1, (r + 1) % 3, 1)
    for r in range(3):
        k1, k2 = 1 << ((r + 1) % 3), 1 << ((r + 2) % 3)
        add_half(r, k2, 0)
        add_half(r, k2, 1)
        send_half(r, k2, (r + 2) % 3, 2)
    sums[pl.ds(0, 16), :] = row_result(ITERS, row_copies)
    own_a = x % 2 + 2 * (y % 2) + 4 * (z % 2)
    near_rows = sums[pl.ds(pl.multiple_of((own_a // 4) * 8, 8), 8), :]
    mine = near_rows[0:2]
    for k in range(1, 4):
        mine = jnp.where(own_a % 4 == k, near_rows[2 * k : 2 * k + 2], mine)
    column = jnp.transpose(jnp.broadcast_to(1.0 / mine[:, None, :], (2, 128, 256)).reshape(256, 256))
    for r in range(3):
        for order in range(3):
            add_half(r, 0, order)
    for i in range(2):
        inverse = column[:, i * 128 : i * 128 + 1]
        mapped_ref[i] = (numer[i] * inverse).astype(bf16)
    for copy in halves:
        copy.wait_send()


def listing(T, partners, counts):
    core, (x, y, z) = place()
    m = jnp.arange(8, dtype=jnp.int32)
    chip = (y ^ ((m >> 1) & 1)) * 16 + (x ^ (m & 1)) * 4 + (z ^ (m >> 2))
    rows = (chip[:, None] * 4 + 2 * core + jnp.arange(2, dtype=jnp.int32)[None, :]).reshape(16)
    named = jnp.take(partners, rows, axis=0)
    limit = jnp.take(counts, rows, axis=0)
    owner = named // 4
    ox, oy, oz = (owner // 4) % 4, owner // 16, owner % 4

    def near(p, q):
        return (p == q) | (p == 3 - q)

    active = near(ox, x) & near(oy, y) & near(oz, z)
    active &= jnp.arange(32, dtype=jnp.int32)[None, :] < limit[:, None]
    jb = ox // 2 + 2 * (oy // 2) + 4 * (oz // 2)
    pick = jnp.max(
        jnp.where(active[:, :, None] & (jb[:, :, None] == m), (named % 4 + 1)[:, :, None], 0), axis=1
    ).reshape(128)
    e = jnp.arange(128, dtype=jnp.int32)
    used = pick > 0
    before = jnp.sum((used[:, None] & (e[:, None] < e[None, :])).astype(jnp.int32), axis=0)
    total = jnp.sum(used.astype(jnp.int32))
    t = jnp.arange(T, dtype=jnp.int32)
    hot = (before[None, :] == t[:, None]) & used[None, :]
    own_a = (x % 2) + 2 * (y % 2) + 4 * (z % 2)
    own_b = (x // 2) + 2 * (y // 2) + 4 * (z // 2)
    a_rel = e // 8
    a_abs = ((e // 16) ^ own_a) * 2 + a_rel % 2
    b_abs = (e % 8) * 4 + jnp.maximum(pick - 1, 0)
    b_rel = ((e % 8) ^ own_b) * 4 + jnp.maximum(pick - 1, 0)

    def chosen(values):
        return jnp.sum(jnp.where(hot, values[None, :], 0), axis=1)

    where = jnp.where(used, before, 0)
    idx = jnp.concatenate([chosen(a_rel), chosen(b_rel), where, b_rel]).astype(jnp.int32)
    shift = jnp.where(t < total, GAIN, 1e30).astype(f32)
    a_t, b_t = chosen(a_abs), chosen(b_abs)
    oa = (a_t[None, :] == jnp.arange(16)[:, None]).astype(bf16)
    ob = (b_t[None, :] == jnp.arange(32)[:, None]).astype(bf16)
    oat = (a_t[:, None] == jnp.arange(16)[None, :]).astype(bf16)
    obt = (b_t[:, None] == jnp.arange(32)[None, :]).astype(bf16)
    obd = ((b_abs[:, None] == jnp.arange(32)[None, :]) & used[:, None]).astype(bf16)
    return idx, shift, oa, oat, ob, obt, obd


def transport(T, cid, own, partners, counts):
    idx, shift, oa, oat, ob, obt, obd = listing(T, partners, counts)
    smem = pl.BlockSpec(memory_space=pltpu.SMEM)
    vmem = pl.BlockSpec(memory_space=pltpu.VMEM)
    dma = pltpu.SemaphoreType.DMA
    return pl.pallas_call(
        functools.partial(kernel, T),
        out_shape=(jax.ShapeDtypeStruct((2, 256, 256), bf16), jax.ShapeDtypeStruct((4, 256), f32)),
        in_specs=[
            smem, smem, pl.BlockSpec(memory_space=pl.ANY), vmem, vmem, vmem, vmem, vmem,
        ],
        out_specs=(vmem, vmem),
        scratch_shapes=[
            pltpu.VMEM((16, 256, 256), bf16),
            pltpu.VMEM((32, 256, 256), bf16),
            pltpu.VMEM((T, 256, 256), bf16),
            pltpu.VMEM((16, 256, 1), f32),
            pltpu.VMEM((32, 8, 256), f32),
            pltpu.VMEM((T, 256), f32),
            pltpu.VMEM((T, 256), f32),
            pltpu.VMEM((128, 256), f32),
            pltpu.VMEM((4, 16, 256), bf16),
            pltpu.VMEM((3, 32, 256), bf16),
            pltpu.VMEM((4, 8, 16, 256), bf16),
            pltpu.VMEM((3, 16, 32, 256), bf16),
            pltpu.VMEM((16, 256, 256), f32),
            pltpu.VMEM((16, 256, 256), bf16),
            pltpu.VMEM((3, 16, 256, 256), bf16),
            dma((1,)),
            dma((2,)),
            dma((2, 3, 8)),
            dma((1,)),
            dma((3,)),
            dma((2, 4)),
            dma((2, 3)),
            dma((3, 3, 8)),
        ],
        compiler_params=pltpu.CompilerParams(
            collective_id=cid, has_side_effects=True, vmem_limit_bytes=60 << 20
        ),
        name=f"transport_{T}",
    )(idx, shift, own, oa, oat, ob, obt, obd)


def most_tiles(partners, counts):
    named = jnp.arange(32, dtype=jnp.int32)[None, :] < counts[:, None]
    owner = partners // 4
    parts = [(owner // 4) % 4, owner // 16, owner % 4]
    kind = sum(((p == 1) | (p == 2)).astype(jnp.int32) * (1 << k) for k, p in enumerate(parts))
    each = jnp.stack([jnp.sum((named & (kind == k)).astype(jnp.int32), axis=1) for k in range(8)])
    return jnp.max(jnp.sum(each.reshape(8, 2, 2, 2, 2, 2, 2, 2, 2), axis=(2, 4, 6, 8)))


def shards(embeds, partners, counts):
    own = embeds.reshape(4, 256, 256)
    mapped, scale = lax.cond(
        most_tiles(partners, counts) <= 64,
        functools.partial(transport, 64, 0),
        functools.partial(transport, 128, 1),
        own,
        partners,
        counts,
    )
    return mapped.reshape(1, 1, 2, 256, 256), scale


def solution(mesh):
    in_specs = (P("side", ("grp", "dev"), None, None), P(), P())
    out_specs = (P(("grp", "dev"), "side", None, None, None), P(("grp", "dev"), None))
    return jax.shard_map(shards, mesh=mesh, in_specs=in_specs, out_specs=out_specs, check_vma=False)
```

profile of v0, /device:TPU:1, one launch (start us, length us, event | category | flops | bytes accessed | tf_op | source)
XLA Modules:
  0.0 121.8 jit_solution(4200774881081093788)
XLA Ops:
  0.6 0.9 convert_reduce_fusion.4
  1.5 0.3 stack.36
  1.8 0.3 stack.37
  2.1 0.3 stack.38
  2.3 0.3 stack.39
  2.6 0.3 stack.40
  2.9 0.3 stack.41
  3.1 0.3 stack.42
  3.4 0.3 stack.43
  3.7 4.1 %stack.35 = s32[8,2,2,2,2,2,2,2,2]{0,8,7,6,5,4,3,2,1:T(2,128)S(1)} concatenate(s32[1,2,2,2,2,2,2,2,2]{0,8,7,6,5,4,3,2,1:T(2,128)S(1)} %stack.36, s32[1,2,2,2,2,2,2,2,2]{0,8,7,6,5,4,3,2,1:T(2,128)S(1)} %stack.37, s32[1,2,2,2,2,2,2,2,2]{0,8,7,6,5,4,3,2,1:T(2,128)S(1)} %stack.38, s32[1,2,2,2,2,2,2,2,2]{0,8,7,6,5,4,3,2,1:T(2,128)S(1)} %stack.39, ...), dimensions={0} | concatenate | bytes 16384 | tf_op jit(solution)/shard_map/stack | solution.py:477
  7.9 0.6 reduce_max.27
  9.2 0.7 copy-done
  9.9 110.6 %conditional.1 = (f32[4,256]{1,0:T(4,128)S(1)}, bf16[1,1,2,256,256]{4,3,2,1,0:T(8,128)(2,1)S(1)}) conditional(s32[]{:T(128)} %convert_element_type.85, (s32[256,32]{0,1:T(8,128)S(1)}, s32[256]{0:T(256)S(1)}, bf16[4,256,256]{2,1,0:T(8,128)(2,1)S(1)}) %tuple.71, (s32[256,32]{0,1:T(8,128)S(1)}, s32[256]{0:T(256)S(1)}, ...), branch_computations={%region_10.20_spmd, %region_18.28_spmd} | conditional | flops 382455 | bytes 141192 | solution.py:483
  10.1 0.7 gather_fusion.3
  10.8 0.1 copy.42
  10.9 0.6 gather_fusion.2
  11.4 0.1 fusion.50
  11.5 0.1 fusion.43
  11.7 0.3 select_reduce_fusion.5
  12.0 0.7 convert_reduce_fusion.3
  12.8 0.1 convert_reduce_fusion.2
  13.0 0.7 fusion.34.obd
  13.7 0.1 select_reduce_fusion.6
  13.9 0.7 fusion.36.oat
  14.5 0.7 fusion.37.obt
  15.2 0.6 fusion.38.ob
  15.8 0.6 fusion.54.oa
  16.4 0.6 pad_add_fusion.1.idx
  17.1 1.1 compare_select_fusion.7.shift
  18.2 102.3 %transport_64.1 = (bf16[2,256,256]{2,1,0:T(8,128)(2,1)S(1)}, f32[4,256]{1,0:T(4,128)S(1)}) custom-call(s32[384]{0:T(512)} %pad_add_fusion.1.idx, f32[64]{0:T(128)} %compare_select_fusion.7.shift, bf16[4,256,256]{2,1,0:T(8,128)(2,1)S(1)} %get-tuple-element.26.x_ref, bf16[16,64]{1,0:T(8,128)(2,1)} %fusion.54.oa, bf16[64,16]{1,0:T(8,128)(2,1)} %fusion.36.oat, ...), custom_call_target="tpu_custom_call" | custom-call | tf_op jit(solution)/shard_map/cond/branch_1_fun/transport_64/pallas_call | solution.py:433
  120.5 0.7 copy.49
  121.2 0.6 copy.50
  (16 shorter events, 0.5 us)
Async XLA Ops:
  3.7 5.6 %copy-start.1 = (bf16[1,4,256,256]{3,2,1,0:T(8,128)(2,1)S(1)}, bf16[1,4,256,256]{3,2,1,0:T(8,128)(2,1)}, u32[]{:S(2)}) copy-start(bf16[1,4,256,256]{3,2,1,0:T(8,128)(2,1)} %param.9) | copy-start | bytes 1572868
  7.8 1.4 %copy-start.2 = (s32[256,32]{0,1:T(8,128)S(1)}, s32[256,32]{0,1:T(8,128)}, u32[]{:S(2)}) copy-start(s32[256,32]{0,1:T(8,128)} %param.10) | copy-start | bytes 98308
  9.2 0.7 copy-start
where the time goes:
time: 122 us
  Pallas kernels  102 us (84%)
  local copies, waits for them, and re-layouts  9.76 us (8%)
  other arithmetic  8.28 us (7%)
  between operations  1.4 us (1%)
    pallas_call x1, Pallas kernels, transport(): pl.pallas_call(functools.partial(kernel, T), out_shape=(jax.ShapeDtypeStr...  102 us
    another operation x9, local copies, waits for them, and re-layouts, most_tiles(): jnp.stack([jnp.sum((named & (kind == k)).astype(jnp.int32), axis=1) for k...  6.2 us

commit v1 on v0

v1 whole, which is shorter than its diff:
```python
import functools
import math

import jax
import jax.numpy as jnp
from jax import lax
from jax.experimental import pallas as pl
from jax.experimental.pallas import tpu as pltpu
from jax.sharding import PartitionSpec as P

ITERS = 3
GAIN = 20.0 * math.log2(math.e)
MESH = pl.DeviceIdType.MESH
NT = (((1,), (1,)), ((), ()))
f32 = jnp.float32
bf16 = jnp.bfloat16
PIECES = ((0, 96), (96, 80), (176, 80))


def place():
    d = lax.axis_index("dev")
    return lax.axis_index("side"), (d // 4, lax.axis_index("grp"), d % 4)


def flip_a(p):
    return p + 1 - 2 * (p % 2)


def flip_b(p):
    return 3 - p


def member(at, flip, bits, core):
    x, y, z = [flip(p) if (bits >> k) & 1 else p for k, p in enumerate(at)]
    return (core, y, x * 4 + z)


def dot(a, b):
    return jnp.dot(a, b, preferred_element_type=f32)


def dot_nt(a, b):
    return lax.dot_general(a, b, NT, preferred_element_type=f32)


def split_dot(onehot, values):
    high = values.astype(bf16)
    low = (values - high.astype(f32)).astype(bf16)
    return dot(onehot, high) + dot(onehot, low)


def kernel(
    T,
    x_ref,
    partners_ref,
    counts_ref,
    mapped_ref,
    scale_ref,
    most_ref,
    oa,
    oat,
    ob,
    obt,
    obd,
    index,
    idx,
    final,
    abuf,
    bbuf,
    tiles,
    row_norm,
    col_norm,
    sums,
    spread,
    dense,
    row_send,
    col_send,
    row_recv,
    col_recv,
    numer,
    ship,
    landed,
    own_sem,
    sib_sem,
    gather_sem,
    relay_sem,
    out_sem,
    row_sem,
    col_sem,
    half_sem,
    index_sem,
):
    core, at = place()
    other = 1 - core
    sibling = member(at, flip_a, 0, other)
    flips = (flip_a, flip_b)
    bufs = (abuf, bbuf)

    barrier = pltpu.get_barrier_semaphore()
    greeted = [sibling]
    for m in range(1, 8):
        greeted += [member(at, flip_a, m, core), member(at, flip_b, m, core), member(at, flip_b, m, other)]
    for peer in greeted:
        pl.semaphore_signal(barrier, inc=1, device_id=peer, device_id_type=MESH)
    pl.semaphore_wait(barrier, len(greeted))

    def remote(src, dst, send, recv, peer):
        return pltpu.make_async_remote_copy(
            src_ref=src, dst_ref=dst, send_sem=send, recv_sem=recv, device_id=peer, device_id_type=MESH
        )

    def unit(cat, slot, piece):
        start, size = PIECES[piece]
        if cat == 0:
            return abuf.at[pl.ds(slot * 2, 2), pl.ds(start, size)]
        return bbuf.at[slot, pl.ds(core * 2, 2), pl.ds(start, size)]

    def unit_copy(cat, dim, piece, slot, src=None):
        there = slot ^ (1 << dim)
        return remote(
            unit(cat, slot, piece) if src is None else src,
            unit(cat, there, piece),
            out_sem.at[0],
            gather_sem.at[cat, piece, there],
            member(at, flips[cat], 1 << dim, core),
        )

    def send_unit(cat, dim, piece, slot):
        copy = unit_copy(cat, dim, piece, slot)
        copy.start()
        return copy

    def send_own(cat, src):
        for step in range(3):
            for dim in range(3):
                piece = (dim - step) % 3
                start, size = PIECES[piece]
                unit_copy(cat, dim, piece, 0, None if src is None else src.at[:, pl.ds(start, size)]).start()

    own_a_half, own_b = abuf.at[pl.ds(0, 2)], bbuf.at[0]

    @pl.when(core == 0)
    def _():
        give = remote(x_ref.at[pl.ds(2, 2)], own_a_half, sib_sem.at[0], sib_sem.at[1], sibling)
        give.start()
        send_own(0, x_ref.at[pl.ds(0, 2)])
        mine = pltpu.make_async_copy(x_ref.at[pl.ds(0, 2)], own_a_half, own_sem.at[0])
        mine.start()
        mine.wait()
        give.wait_send()
        pltpu.make_async_copy(own_b, own_b, sib_sem.at[1]).wait()
        send_own(1, None)

    @pl.when(core == 1)
    def _():
        give = remote(x_ref, own_b, sib_sem.at[0], sib_sem.at[1], sibling)
        give.start()
        send_own(1, x_ref.at[pl.ds(2, 2)])
        mine = pltpu.make_async_copy(x_ref, own_b, own_sem.at[0])
        mine.start()
        mine.wait()
        give.wait_send()
        pltpu.make_async_copy(own_a_half, own_a_half, sib_sem.at[1]).wait()
        send_own(0, None)

    sent = []
    relays = []

    def arrived(cat, piece, slot):
        here = unit(cat, slot, piece)
        pltpu.make_async_copy(here, here, gather_sem.at[cat, piece, slot]).wait()
        if cat == 1:
            copy = remote(here, here, out_sem.at[1], relay_sem.at[slot], sibling)
            copy.start()
            relays.append(copy)

    def iota(shape, dim):
        return lax.broadcasted_iota(jnp.int32, shape, dim)

    diagonal = iota((128, 128), 0) == iota((128, 128), 1)

    def norms(slot):
        if slot:
            here = bbuf.at[slot, pl.ds(other * 2, 2)]
            pltpu.make_async_copy(here, here, relay_sem.at[slot]).wait()

        def a_body(i, c):
            x = abuf[slot * 2 + i].astype(f32)
            total = jnp.sum(x * x, axis=1, keepdims=True)
            row_norm[slot * 2 + i] = lax.rsqrt(total * (1.0 / 256.0) + 1e-06) * (GAIN / 16.0)
            return c

        def b_body(i, c):
            for h in range(2):
                y = bbuf[slot, i, pl.ds(h * 128, 128), :]
                total = jnp.sum(jnp.where(diagonal, dot_nt(y, y), 0.0), axis=0, keepdims=True)
                norm = lax.rsqrt(total * (1.0 / 256.0) + 1e-06) * (1.0 / 16.0)
                col_norm[slot * 4 + i, :, pl.ds(h * 128, 128)] = jnp.broadcast_to(norm, (8, 128))
            return c

        lax.fori_loop(0, 2, a_body, 0)
        lax.fori_loop(0, 4, b_body, 0)

    def bits_of(values, shifts):
        return [(values >> k) & 1 for k in shifts]

    def flipped(bits, by):
        return sum((b + f - 2 * b * f) * (1 << k) for k, (b, f) in enumerate(zip(bits, by)))

    def make_list():
        x, y, z = at
        own_low = [p % 2 for p in at]
        own_high = [p // 2 for p in at]
        named_all = partners_ref[...]
        limit_row = counts_ref[...]
        r = iota((16, 256), 0)
        cx, cy, cz = [flipped([b], [p % 2]) + 2 * (p // 2) for b, p in zip(bits_of(r, (1, 2, 3)), at)]
        chosen = iota((16, 256), 1) == (cy * 16 + cx * 4 + cz) * 4 + 2 * core + (r & 1)
        named = dot(chosen.astype(f32).astype(bf16), named_all.astype(f32).astype(bf16)).astype(jnp.int32)
        limit = jnp.sum(jnp.where(chosen, jnp.broadcast_to(limit_row, (16, 256)), 0).astype(f32), axis=1, keepdims=True)
        slot_at = iota((16, 32), 1).astype(f32)

        def coords(entry):
            owner = entry >> 2
            return (owner >> 2) & 3, owner >> 4, owner & 3

        parts = coords(named)
        active = slot_at < limit
        for p, q in zip(parts, at):
            active &= (p == q) | (p == 3 - q)
        jb = sum((p >> 1) * (1 << k) for k, p in enumerate(parts))
        pick = (named & 3) + 1
        lane = iota((16, 128), 1)
        bp = jnp.zeros((16, 128), f32)
        for k in range(8):
            best = jnp.max(jnp.where(active & (jb == k), pick, 0).astype(f32), axis=1, keepdims=True)
            bp = jnp.where(lane == k, best, bp)
        used = jnp.where(bp > 0, 1.0, 0.0).astype(bf16)
        i128, j128 = iota((128, 128), 0), iota((128, 128), 1)

        def mask(m):
            return jnp.where(m, 1.0, 0.0).astype(bf16)

        in_row = dot(used, mask(i128 < j128))
        of_row = dot(used, mask(i128 < 128))
        above = dot(mask(iota((16, 16), 1) < iota((16, 16), 0)), of_row.astype(bf16))
        pos = above + in_row
        k3 = bits_of(lane, (0, 1, 2))
        b_rel = flipped(k3, own_high) * 4 + jnp.maximum(bp.astype(jnp.int32) - 1, 0)
        index[pl.ds(0, 16), :] = jnp.where(bp > 0, jnp.minimum(pos, T - 1.0), 0.0).astype(jnp.int32)
        index[pl.ds(16, 16), :] = jnp.where(lane < 8, b_rel, 0)

        spread_out = mask(i128 == (j128 & 7))
        own_lane = (lane >> 3) == iota((16, 128), 0)

        def flat(values):
            return jnp.sum(jnp.where(own_lane, dot(values.astype(bf16), spread_out), 0.0), axis=0, keepdims=True)

        bp_row, pos_row = flat(bp), flat(pos)
        hot = mask((iota((T, 128), 0).astype(f32) == pos_row) & (bp_row > 0))
        e = iota((8, 128), 1)
        pick_row = jnp.maximum(jnp.broadcast_to(bp_row, (8, 128)).astype(jnp.int32) - 1, 0)
        b_e = flipped(bits_of(e, (0, 1, 2)), own_high) * 4 + pick_row
        values = jnp.where(iota((8, 128), 0) == 0, e >> 3, b_e).astype(f32).astype(bf16)
        index[pl.ds(32, 8), pl.ds(0, T)] = dot_nt(values, hot).astype(jnp.int32)
        fetch = pltpu.make_async_copy(index, idx, index_sem.at[0])
        fetch.start()
        e16, e32 = iota((16, 128), 1), iota((32, 128), 1)
        a_abs = flipped(bits_of(e16, (4, 5, 6)), own_low) * 2 + ((e16 >> 3) & 1)
        a_hot = mask(iota((16, 128), 0) == a_abs)
        b_abs = (e32 & 7) * 4 + jnp.broadcast_to(bp_row, (32, 128)).astype(jnp.int32) - 1
        b_hot = mask((iota((32, 128), 0) == b_abs) & (bp_row > 0))
        oa[...] = dot_nt(a_hot, hot).astype(bf16)
        oat[...] = dot_nt(hot, a_hot).astype(bf16)
        ob[...] = dot_nt(b_hot, hot).astype(bf16)
        obt[...] = dot_nt(hot, b_hot).astype(bf16)
        obd[...] = dot_nt(mask(i128 == j128), b_hot).astype(bf16)

        limit_all = jnp.transpose(jnp.broadcast_to(limit_row.astype(f32), (128, 256)))[:, 0:32]
        active = iota((256, 32), 1).astype(f32) < limit_all
        kind = sum((((p + 1) >> 1) & 1) * (1 << k) for k, p in enumerate(coords(named_all)))
        g, row = iota((16, 256), 0), iota((16, 256), 1)
        group = ((row >> 7) & 1) * 8 + ((row >> 5) & 1) * 4 + ((row >> 3) & 1) * 2 + ((row >> 1) & 1)
        members = mask(g == group)
        most = jnp.zeros((16, 1), f32)
        for k in range(8):
            most = jnp.maximum(
                most, jnp.sum(dot(members, mask(active & (kind == k))), axis=1, keepdims=True)
            )
        most_ref[...] = jnp.broadcast_to(jnp.max(most, axis=0, keepdims=True), (8, 128))
        fetch.wait()

    def received(steps):
        for r in range(3):
            slot = steps(1 << r, 1 << ((r + 1) % 3), 1 << ((r + 2) % 3))
            for cat in range(2):
                arrived(cat, r, slot)
                yield cat, r, slot

    for cat, r, slot in received(lambda k0, k1, k2: k0):
        sent.append(send_unit(cat, (r + 1) % 3, r, slot))
    for r in range(3):
        for cat in range(2):
            sent.append(send_unit(cat, (r + 2) % 3, r, 1 << r))
    norms(0)
    for cat, r, slot in received(lambda k0, k1, k2: k1):
        sent.append(send_unit(cat, (r + 2) % 3, r, slot))
    make_list()
    for _ in received(lambda k0, k1, k2: k2):
        pass
    for cat, r, slot in received(lambda k0, k1, k2: k0 | k1):
        sent.append(send_unit(cat, (r + 2) % 3, r, slot))
    for slot in (1, 2, 4):
        norms(slot)
    for _ in received(lambda k0, k1, k2: k2 | k0):
        pass
    for _ in received(lambda k0, k1, k2: k2 | k1):
        pass
    for slot in (3, 5, 6):
        norms(slot)
    for _ in received(lambda k0, k1, k2: 7):
        pass
    norms(7)
    for cat in range(2):
        for step in range(3):
            for dim in range(3):
                sent.append(unit_copy(cat, dim, (dim - step) % 3, 0))
    for copy in sent:
        copy.wait_send()
    for copy in relays:
        copy.wait_send()
    ones = jnp.ones((8, 256), bf16)

    row_id = lax.broadcasted_iota(jnp.int32, (8, 256), 0)

    def build(i, c):
        total = jnp.zeros((8, 256), f32)
        for u in range(8):
            t = i * 8 + u
            a, b = jnp.clip(idx[32, t], 0, 15), jnp.clip(idx[33, t], 0, 31)
            scores = dot_nt(abuf[a], bbuf[b // 4, b % 4])
            tile = jnp.exp2(scores * row_norm[a] * col_norm[b][0:1] - GAIN).astype(bf16)
            tiles[t] = tile
            total = jnp.where(row_id == u, dot_nt(ones, tile), total)
        sums[pl.ds(pl.multiple_of(i * 8, 8), 8), :] = total
        return c

    lax.fori_loop(0, T // 8, build, 0)

    def sweep(transposed):
        def body(i, c):
            rows = pl.ds(pl.multiple_of(i * 8, 8), 8)
            left = spread[rows, :].astype(bf16)
            total = jnp.zeros((8, 256), f32)
            for u in range(8):
                tile = tiles[i * 8 + u]
                part = dot_nt(left, tile) if transposed else dot(left, tile)
                total = jnp.where(row_id == u, part, total)
            sums[rows, :] = total
            return c

        lax.fori_loop(0, T // 8, body, 0)

    def row_exchange(phase, partial):
        row_send[phase] = partial.astype(bf16)
        copies = []
        for m in range(1, 8):
            copy = remote(
                row_send.at[phase], row_recv.at[phase, m], row_sem.at[0, phase], row_sem.at[1, phase],
                member(at, flip_a, m, core),
            )
            copy.start()
            copies.append(copy)
        return copies

    def row_result(phase, copies):
        got = row_recv.at[phase, pl.ds(1, 7)]
        pltpu.make_async_copy(got, got, row_sem.at[1, phase]).wait()
        total = row_send[phase].astype(f32)
        for m in range(1, 8):
            total += row_recv[phase, m].astype(f32)
        for copy in copies:
            copy.wait_send()
        return total

    def col_exchange(phase):
        col_send[phase] = split_dot(ob[...], sums[...]).astype(bf16)
        copies = []
        for far in range(2):
            for m in range(8):
                if far + m:
                    copy = remote(
                        col_send.at[phase], col_recv.at[phase, far * 8 + m], col_sem.at[0, phase],
                        col_sem.at[1, phase], member(at, flip_b, m, other if far else core),
                    )
                    copy.start()
                    copies.append(copy)
        got = col_recv.at[phase, pl.ds(1, 15)]
        pltpu.make_async_copy(got, got, col_sem.at[1, phase]).wait()
        total = col_send[phase].astype(f32)
        for m in range(1, 16):
            total += col_recv[phase, m].astype(f32)
        for copy in copies:
            copy.wait_send()
        return total

    for phase in range(ITERS):
        if phase:
            sweep(True)
        scale_a = 1.0 / row_result(phase, row_exchange(phase, split_dot(oa[...], sums[...])))
        spread[...] = dot(oat[...], scale_a.astype(bf16))
        sweep(False)
        scale_b = 1.0 / (1.0 + col_exchange(phase))
        spread[...] = dot(obt[...], scale_b.astype(bf16))
    x, y, z = at
    member_b = x // 2 + 2 * (y // 2) + 4 * (z // 2)
    sums[pl.ds(0, 32), :] = scale_b
    near_rows = sums[pl.ds(pl.multiple_of((member_b // 2) * 8, 8), 8), :]
    scale_ref[...] = jnp.where(member_b % 2 == 0, near_rows[0:4], near_rows[4:8])
    dense[...] = dot(obd[...], scale_b.astype(bf16))

    def partial(slot):
        def body(i, c):
            total, mass = None, None
            a = slot * 2 + i
            rows = dense[pl.ds(pl.multiple_of(a * 8, 8), 8), :]
            for d in range(8):
                weights = tiles[jnp.clip(idx[a, d], 0, T - 1)].astype(f32) * rows[d : d + 1]
                b = jnp.clip(idx[16 + a, d], 0, 31)
                part = dot(weights.astype(bf16), bbuf[b // 4, b % 4])
                half = weights[:, 0:128] + weights[:, 128:256]
                total = part if total is None else total + part
                mass = half if mass is None else mass + half
            numer[a] = total
            column = jnp.sum(mass, axis=1, keepdims=True)
            a_at = flipped([(slot >> k) & 1 for k in range(3)], [p % 2 for p in at]) * 2 + i
            final[...] = jnp.where(iota((256, 128), 1) == a_at, column, final[...])
            return c

        lax.fori_loop(0, 2, body, 0)

    halves = []
    final[...] = jnp.zeros((256, 128), f32)

    def send_half(piece, slot, dim, order):
        start, size = PIECES[piece]
        two, rows = pl.ds(slot * 2, 2), pl.ds(start, size)
        ship[two, rows, :] = numer[two, rows, :].astype(bf16)
        there = slot ^ (1 << dim)
        copy = remote(
            ship.at[two, rows], landed.at[order, pl.ds(there * 2, 2), rows], out_sem.at[2], half_sem.at[order, piece, there],
            member(at, flip_a, 1 << dim, core),
        )
        copy.start()
        halves.append(copy)

    def add_half(piece, slot, order):
        start, size = PIECES[piece]
        two, rows = pl.ds(slot * 2, 2), pl.ds(start, size)
        here = landed.at[order, two, rows]
        pltpu.make_async_copy(here, here, half_sem.at[order, piece, slot]).wait()
        numer[two, rows, :] = numer[two, rows, :] + landed[order, two, rows, :].astype(f32)

    for slot in (7, 3, 5, 6, 1, 2, 4, 0):
        partial(slot)
        for r in range(3):
            if (slot >> r) & 1:
                send_half(r, slot, r, 0)
    for r in range(3):
        k1, k2 = 1 << ((r + 1) % 3), 1 << ((r + 2) % 3)
        add_half(r, k1 | k2, 0)
        send_half(r, k1 | k2, (r + 1) % 3, 1)
    row_copies = row_exchange(ITERS, jnp.transpose(final[...])[0:16])
    for r in range(3):
        k1, k2 = 1 << ((r + 1) % 3), 1 << ((r + 2) % 3)
        add_half(r, k1, 0)
        send_half(r, k1, (r + 1) % 3, 1)
    for r in range(3):
        k1, k2 = 1 << ((r + 1) % 3), 1 << ((r + 2) % 3)
        add_half(r, k2, 0)
        add_half(r, k2, 1)
        send_half(r, k2, (r + 2) % 3, 2)
    sums[pl.ds(0, 16), :] = row_result(ITERS, row_copies)
    own_a = x % 2 + 2 * (y % 2) + 4 * (z % 2)
    near_rows = sums[pl.ds(pl.multiple_of((own_a // 4) * 8, 8), 8), :]
    mine = near_rows[0:2]
    for k in range(1, 4):
        mine = jnp.where(own_a % 4 == k, near_rows[2 * k : 2 * k + 2], mine)
    column = jnp.transpose(jnp.broadcast_to(1.0 / mine[:, None, :], (2, 128, 256)).reshape(256, 256))
    for r in range(3):
        for order in range(3):
            add_half(r, 0, order)
    for i in range(2):
        inverse = column[:, i * 128 : i * 128 + 1]
        mapped_ref[i] = (numer[i] * inverse).astype(bf16)
    for copy in halves:
        copy.wait_send()


def transport(T, cid, own, partners, counts):
    vmem = pl.BlockSpec(memory_space=pltpu.VMEM)
    dma = pltpu.SemaphoreType.DMA
    return pl.pallas_call(
        functools.partial(kernel, T),
        out_shape=(
            jax.ShapeDtypeStruct((2, 256, 256), bf16),
            jax.ShapeDtypeStruct((4, 256), f32),
            jax.ShapeDtypeStruct((8, 128), f32),
        ),
        in_specs=[pl.BlockSpec(memory_space=pl.ANY), vmem, vmem],
        out_specs=(vmem, vmem, vmem),
        scratch_shapes=[
            pltpu.VMEM((16, T), bf16),
            pltpu.VMEM((T, 16), bf16),
            pltpu.VMEM((32, T), bf16),
            pltpu.VMEM((T, 32), bf16),
            pltpu.VMEM((128, 32), bf16),
            pltpu.VMEM((40, 128), jnp.int32),
            pltpu.SMEM((40, 128), jnp.int32),
            pltpu.VMEM((256, 128), f32),
            pltpu.VMEM((16, 256, 256), bf16),
            pltpu.VMEM((8, 4, 256, 256), bf16),
            pltpu.VMEM((T, 256, 256), bf16),
            pltpu.VMEM((16, 256, 1), f32),
            pltpu.VMEM((32, 8, 256), f32),
            pltpu.VMEM((T, 256), f32),
            pltpu.VMEM((T, 256), f32),
            pltpu.VMEM((128, 256), f32),
            pltpu.VMEM((4, 16, 256), bf16),
            pltpu.VMEM((3, 32, 256), bf16),
            pltpu.VMEM((4, 8, 16, 256), bf16),
            pltpu.VMEM((3, 16, 32, 256), bf16),
            pltpu.VMEM((16, 256, 256), f32),
            pltpu.VMEM((16, 256, 256), bf16),
            pltpu.VMEM((3, 16, 256, 256), bf16),
            dma((1,)),
            dma((2,)),
            dma((2, 3, 8)),
            dma((8,)),
            dma((3,)),
            dma((2, 4)),
            dma((2, 3)),
            dma((3, 3, 8)),
            dma((1,)),
        ],
        compiler_params=pltpu.CompilerParams(
            collective_id=cid, has_side_effects=True, vmem_limit_bytes=60 << 20
        ),
        name=f"transport_{T}",
    )(own, partners, counts)


def shards(embeds, partners, counts):
    args = embeds.reshape(4, 256, 256), partners, counts.reshape(1, 256)
    mapped, scale, most = transport(64, 0, *args)
    mapped, scale = lax.cond(
        most[0, 0] <= 64.0,
        lambda mapped, scale, *args: (mapped, scale),
        lambda mapped, scale, *args: transport(128, 1, *args)[:2],
        mapped,
        scale,
        *args,
    )
    return mapped.reshape(1, 1, 2, 256, 256), scale


def solution(mesh):
    in_specs = (P("side", ("grp", "dev"), None, None), P(), P())
    out_specs = (P(("grp", "dev"), "side", None, None, None), P(("grp", "dev"), None))
    return jax.shard_map(shards, mesh=mesh, in_specs=in_specs, out_specs=out_specs, check_vma=False)
```

time: 122 us -> 106 us (0.87)
  other arithmetic: 8.28 us -> 0 us
  local copies, waits for them, and re-layouts: 9.76 us -> 4.71 us
  Pallas kernels: 102 us -> 99.5 us
    another operation x10 -> x0, local copies, waits for them, and re-layouts: 6.3 us -> none  [the longest x9 6.2 us: most_tiles(): jnp.stack([jnp.sum((named & (kind == k)).astype(jnp.int32), axis=1) for k...]
    convert_element_type x5 -> x0, other arithmetic: 3.27 us -> none  [the longest x1 0.72 us: listing(): ((b_abs[:, None] == jnp.arange(32)[None, :]) & used[:, None]).astype(bf16)]
    pallas_call x1, Pallas kernels: 102 us -> 99.5 us  [transport(): pl.pallas_call(functools.partial(kernel, T), out_shape=(jax.ShapeDtypeStr...]
    reduce_sum x5 -> x0, other arithmetic: 1.91 us -> none  [the longest x1 0.92 us: most_tiles(): jnp.sum((named & (kind == k)).astype(jnp.int32), axis=1)]
    unnamed x8 -> x9, local copies, waits for them, and re-layouts: 1.96 us -> 3.53 us
    gather x2 -> x0, local copies, waits for them, and re-layouts: 1.23 us -> none  [the longest x1 0.67 us: listing(): limit = jnp.take(counts, rows, axis=0)]
where the time goes in v1:
time: 106 us
  Pallas kernels  99.5 us (94%)
  local copies, waits for them, and re-layouts  4.71 us (4%)
  between operations  1.33 us (1%)
    pallas_call x1, Pallas kernels, transport(): pl.pallas_call(functools.partial(kernel, T), out_shape=(jax.ShapeDtypeStr...  99.5 us
    unnamed x9, local copies, waits for them, and re-layouts  3.53 us

profile of v1, /device:TPU:1, one launch (start us, length us, event | category | flops | bytes accessed | tf_op | source)
XLA Modules:
  0.0 105.5 jit_solution(6814186979972589950)
XLA Ops:
  0.6 0.0 copy-start
  0.6 1.6 %copy.5.partners_ref = s32[256,32]{1,0:T(8,128)} copy(s32[256,32]{0,1:T(8,128)} %param.6) | data formatting | bytes 65536 | tf_op args[1]
  2.2 0.0 copy-start.1
  2.2 99.5 %transport_64.1 = (bf16[2,256,256]{2,1,0:T(8,128)(2,1)S(1)}, f32[4,256]{1,0:T(4,128)S(1)}, f32[8,128]{1,0:T(8,128)}) custom-call(bf16[4,256,256]{2,1,0:T(8,128)(2,1)} %bitcast.4, s32[256,32]{1,0:T(8,128)} %copy.5.partners_ref, s32[1,256]{1,0:T(1,128)} %bitcast.7), custom_call_target="tpu_custom_call" | custom-call | tf_op jit(solution)/shard_map/transport_64/pallas_call | solution.py:503
  101.7 1.2 %slice.3 = f32[1,1]{1,0:T(1,128)} slice(f32[8,128]{1,0:T(8,128)} %get-tuple-element.22), slice={[0:1], [0:1]} | slice | bytes 8 | tf_op jit(solution)/shard_map/slice | solution.py:557
  103.6 0.0 copy-start.2
  103.6 0.0 copy-done
  103.6 0.0 copy-done.1
  103.6 0.7 copy-done.2
  104.3 0.7 copy.13
  105.0 0.6 copy.14
  (1 shorter events, 0.0 us)
Async XLA Ops:
  0.6 103.0 %copy-start = (bf16[1,4,256,256]{3,2,1,0:T(8,128)(2,1)S(1)}, bf16[1,4,256,256]{3,2,1,0:T(8,128)(2,1)}, u32[]{:S(2)}) copy-start(bf16[1,4,256,256]{3,2,1,0:T(8,128)(2,1)} %param.5) | copy-start | bytes 1572868
  2.2 101.4 %copy-start.1 = (s32[256,32]{0,1:T(8,128)S(1)}, s32[256,32]{0,1:T(8,128)}, u32[]{:S(2)}) copy-start(s32[256,32]{0,1:T(8,128)} %param.6) | copy-start | bytes 98308
  103.6 0.7 copy-start.2

commit v2 on v1

--- a/solution.py
+++ b/solution.py
@@ -9,6 +9,7 @@
 from jax.sharding import PartitionSpec as P
 
 ITERS = 3
+TURN = 32
 GAIN = 20.0 * math.log2(math.e)
 MESH = pl.DeviceIdType.MESH
 NT = (((1,), (1,)), ((), ()))
@@ -65,12 +66,16 @@
     index,
     idx,
     final,
+    norms_a,
+    norms_b,
+    norm_sem,
     abuf,
     bbuf,
     tiles,
     row_norm,
     col_norm,
     sums,
+    columns,
     spread,
     dense,
     row_send,
@@ -94,6 +99,7 @@
     other = 1 - core
     sibling = member(at, flip_a, 0, other)
     flips = (flip_a, flip_b)
+    norm_bufs = (norms_a, norms_b)
     bufs = (abuf, bbuf)
 
     barrier = pltpu.get_barrier_semaphore()
@@ -179,27 +185,44 @@
 
     diagonal = iota((128, 128), 0) == iota((128, 128), 1)
 
-    def norms(slot):
-        if slot:
-            here = bbuf.at[slot, pl.ds(other * 2, 2)]
-            pltpu.make_async_copy(here, here, relay_sem.at[slot]).wait()
-
-        def a_body(i, c):
-            x = abuf[slot * 2 + i].astype(f32)
-            total = jnp.sum(x * x, axis=1, keepdims=True)
-            row_norm[slot * 2 + i] = lax.rsqrt(total * (1.0 / 256.0) + 1e-06) * (GAIN / 16.0)
-            return c
-
-        def b_body(i, c):
+    norm_copies = []
+
+    def send_norms():
+        def inverse_norm(block, scale):
+            halves = []
             for h in range(2):
-                y = bbuf[slot, i, pl.ds(h * 128, 128), :]
+                y = block[h * 128 : h * 128 + 128]
                 total = jnp.sum(jnp.where(diagonal, dot_nt(y, y), 0.0), axis=0, keepdims=True)
-                norm = lax.rsqrt(total * (1.0 / 256.0) + 1e-06) * (1.0 / 16.0)
-                col_norm[slot * 4 + i, :, pl.ds(h * 128, 128)] = jnp.broadcast_to(norm, (8, 128))
-            return c
-
-        lax.fori_loop(0, 2, a_body, 0)
-        lax.fori_loop(0, 4, b_body, 0)
+                halves.append(lax.rsqrt(total * (1.0 / 256.0) + 1e-06) * scale)
+            return jnp.concatenate(halves, axis=1)
+
+        for i in range(2):
+            norm_bufs[0][0, i : i + 1] = inverse_norm(abuf[i], GAIN / 16.0)
+        for i in range(4):
+            norm_bufs[1][0, i : i + 1] = inverse_norm(bbuf[0, i], 1.0 / 16.0)
+        for cat in range(2):
+            for m in range(1, 8):
+                copy = remote(
+                    norm_bufs[cat].at[0], norm_bufs[cat].at[m], norm_sem.at[0, cat], norm_sem.at[1, cat],
+                    member(at, flips[cat], m, core),
+                )
+                copy.start()
+                norm_copies.append(copy)
+
+    def take_norms():
+        for cat in range(2):
+            got = norm_bufs[cat].at[pl.ds(1, 7)]
+            pltpu.make_async_copy(got, got, norm_sem.at[1, cat]).wait()
+        for copy in norm_copies:
+            copy.wait_send()
+        flipped_norms = jnp.transpose(
+            jnp.concatenate([norm_bufs[0][m] for m in range(8)] + [jnp.zeros((64, 256), f32)], axis=0)
+        )
+        for a in range(16):
+            lane = (a // 2) * 8 + a % 2
+            row_norm[a] = flipped_norms[:, lane : lane + 1]
+        for b in range(32):
+            col_norm[b] = jnp.broadcast_to(norm_bufs[1][b // 4, b % 4 : b % 4 + 1], (8, 256))
 
     def bits_of(values, shifts):
         return [(values >> k) & 1 for k in shifts]
@@ -216,7 +239,7 @@
         r = iota((16, 256), 0)
         cx, cy, cz = [flipped([b], [p % 2]) + 2 * (p // 2) for b, p in zip(bits_of(r, (1, 2, 3)), at)]
         chosen = iota((16, 256), 1) == (cy * 16 + cx * 4 + cz) * 4 + 2 * core + (r & 1)
-        named = dot(chosen.astype(f32).astype(bf16), named_all.astype(f32).astype(bf16)).astype(jnp.int32)
+        named = dot_nt(chosen.astype(f32).astype(bf16), named_all.astype(f32).astype(bf16)).astype(jnp.int32)
         limit = jnp.sum(jnp.where(chosen, jnp.broadcast_to(limit_row, (16, 256)), 0).astype(f32), axis=1, keepdims=True)
         slot_at = iota((16, 32), 1).astype(f32)
 
@@ -276,8 +299,7 @@
         obt[...] = dot_nt(hot, b_hot).astype(bf16)
         obd[...] = dot_nt(mask(i128 == j128), b_hot).astype(bf16)
 
-        limit_all = jnp.transpose(jnp.broadcast_to(limit_row.astype(f32), (128, 256)))[:, 0:32]
-        active = iota((256, 32), 1).astype(f32) < limit_all
+        active = iota((32, 256), 0) < limit_row
         kind = sum((((p + 1) >> 1) & 1) * (1 << k) for k, p in enumerate(coords(named_all)))
         g, row = iota((16, 256), 0), iota((16, 256), 1)
         group = ((row >> 7) & 1) * 8 + ((row >> 5) & 1) * 4 + ((row >> 3) & 1) * 2 + ((row >> 1) & 1)
@@ -285,9 +307,9 @@
         most = jnp.zeros((16, 1), f32)
         for k in range(8):
             most = jnp.maximum(
-                most, jnp.sum(dot(members, mask(active & (kind == k))), axis=1, keepdims=True)
+                most, jnp.sum(dot_nt(members, mask(active & (kind == k))), axis=1, keepdims=True)
             )
-        most_ref[...] = jnp.broadcast_to(jnp.max(most, axis=0, keepdims=True), (8, 128))
+        most_ref[0, 0] = jnp.max(most)
         fetch.wait()
 
     def received(steps):
@@ -297,30 +319,26 @@
                 arrived(cat, r, slot)
                 yield cat, r, slot
 
+    send_norms()
     for cat, r, slot in received(lambda k0, k1, k2: k0):
         sent.append(send_unit(cat, (r + 1) % 3, r, slot))
     for r in range(3):
         for cat in range(2):
             sent.append(send_unit(cat, (r + 2) % 3, r, 1 << r))
-    norms(0)
     for cat, r, slot in received(lambda k0, k1, k2: k1):
         sent.append(send_unit(cat, (r + 2) % 3, r, slot))
     make_list()
+    for cat, r, slot in received(lambda k0, k1, k2: k0 | k1):
+        sent.append(send_unit(cat, (r + 2) % 3, r, slot))
     for _ in received(lambda k0, k1, k2: k2):
         pass
-    for cat, r, slot in received(lambda k0, k1, k2: k0 | k1):
-        sent.append(send_unit(cat, (r + 2) % 3, r, slot))
-    for slot in (1, 2, 4):
-        norms(slot)
+    take_norms()
     for _ in received(lambda k0, k1, k2: k2 | k0):
         pass
     for _ in received(lambda k0, k1, k2: k2 | k1):
         pass
-    for slot in (3, 5, 6):
-        norms(slot)
     for _ in received(lambda k0, k1, k2: 7):
         pass
-    norms(7)
     for cat in range(2):
         for step in range(3):
             for dim in range(3):
@@ -329,37 +347,65 @@
         copy.wait_send()
     for copy in relays:
         copy.wait_send()
-    ones = jnp.ones((8, 256), bf16)
-
-    row_id = lax.broadcasted_iota(jnp.int32, (8, 256), 0)
+    for slot in range(1, 8):
+        here = bbuf.at[slot, pl.ds(other * 2, 2)]
+        pltpu.make_async_copy(here, here, relay_sem.at[slot]).wait()
 
     def build(i, c):
-        total = jnp.zeros((8, 256), f32)
-        for u in range(8):
-            t = i * 8 + u
+        for u in range(TURN):
+            t = i * TURN + u
             a, b = jnp.clip(idx[32, t], 0, 15), jnp.clip(idx[33, t], 0, 31)
             scores = dot_nt(abuf[a], bbuf[b // 4, b % 4])
-            tile = jnp.exp2(scores * row_norm[a] * col_norm[b][0:1] - GAIN).astype(bf16)
-            tiles[t] = tile
-            total = jnp.where(row_id == u, dot_nt(ones, tile), total)
-        sums[pl.ds(pl.multiple_of(i * 8, 8), 8), :] = total
+            tiles[t] = jnp.exp2(scores * row_norm[a] * col_norm[b][0:1] - GAIN).astype(bf16)
         return c
 
-    lax.fori_loop(0, T // 8, build, 0)
-
-    def sweep(transposed):
+    lax.fori_loop(0, T // TURN, build, 0)
+
+    row_id = iota((8, 256), 0)
+    lane_id = iota((256, T), 1)
+
+    def row_sweep():
         def body(i, c):
-            rows = pl.ds(pl.multiple_of(i * 8, 8), 8)
-            left = spread[rows, :].astype(bf16)
-            total = jnp.zeros((8, 256), f32)
-            for u in range(8):
-                tile = tiles[i * 8 + u]
-                part = dot_nt(left, tile) if transposed else dot(left, tile)
-                total = jnp.where(row_id == u, part, total)
-            sums[rows, :] = total
+            beside = columns[...]
+            for g in range(TURN // 8):
+                base = i * TURN + g * 8
+                rows = pl.ds(pl.multiple_of(base, 8), 8)
+                left = spread[rows, :]
+                left_bf = left.astype(bf16)
+                total = jnp.zeros((8, 256), f32)
+                for u in range(8):
+                    tile = tiles[base + u]
+                    if u % 2 == 0:
+                        total = jnp.where(row_id == u, dot_nt(left_bf, tile), total)
+                    else:
+                        scaled = tile.astype(f32) * left[u : u + 1]
+                        mass = jnp.sum(scaled[:, 0:128] + scaled[:, 128:256], axis=1, keepdims=True)
+                        beside = jnp.where(lane_id == base + u, mass, beside)
+                sums[rows, :] = total
+            columns[...] = beside
             return c
 
-        lax.fori_loop(0, T // 8, body, 0)
+        columns[...] = jnp.zeros((256, T), f32)
+        lax.fori_loop(0, T // TURN, body, 0)
+        beside = columns[...]
+        high = beside.astype(bf16)
+        low = (beside - high.astype(f32)).astype(bf16)
+        return split_dot(oa[...], sums[...]) + dot_nt(oa[...], high) + dot_nt(oa[...], low)
+
+    def col_sweep():
+        def body(i, c):
+            for g in range(TURN // 8):
+                base = i * TURN + g * 8
+                rows = pl.ds(pl.multiple_of(base, 8), 8)
+                left = spread[rows, :].astype(bf16)
+                total = jnp.zeros((8, 256), f32)
+                for u in range(8):
+                    total = jnp.where(row_id == u, dot(left, tiles[base + u]), total)
+                sums[rows, :] = total
+            return c
+
+        lax.fori_loop(0, T // TURN, body, 0)
+        return split_dot(ob[...], sums[...])
 
     def row_exchange(phase, partial):
         row_send[phase] = partial.astype(bf16)
@@ -383,8 +429,8 @@
             copy.wait_send()
         return total
 
-    def col_exchange(phase):
-        col_send[phase] = split_dot(ob[...], sums[...]).astype(bf16)
+    def col_exchange(phase, partial):
+        col_send[phase] = partial.astype(bf16)
         copies = []
         for far in range(2):
             for m in range(8):
@@ -404,13 +450,11 @@
             copy.wait_send()
         return total
 
+    spread[...] = jnp.ones((T, 256), f32)
     for phase in range(ITERS):
-        if phase:
-            sweep(True)
-        scale_a = 1.0 / row_result(phase, row_exchange(phase, split_dot(oa[...], sums[...])))
+        scale_a = 1.0 / row_result(phase, row_exchange(phase, row_sweep()))
         spread[...] = dot(oat[...], scale_a.astype(bf16))
-        sweep(False)
-        scale_b = 1.0 / (1.0 + col_exchange(phase))
+        scale_b = 1.0 / (1.0 + col_exchange(phase, col_sweep()))
         spread[...] = dot(obt[...], scale_b.astype(bf16))
     x, y, z = at
     member_b = x // 2 + 2 * (y // 2) + 4 * (z // 2)
@@ -505,10 +549,10 @@
         out_shape=(
             jax.ShapeDtypeStruct((2, 256, 256), bf16),
             jax.ShapeDtypeStruct((4, 256), f32),
-            jax.ShapeDtypeStruct((8, 128), f32),
+            jax.ShapeDtypeStruct((1, 1), f32),
         ),
         in_specs=[pl.BlockSpec(memory_space=pl.ANY), vmem, vmem],
-        out_specs=(vmem, vmem, vmem),
+        out_specs=(vmem, vmem, pl.BlockSpec(memory_space=pltpu.SMEM)),
         scratch_shapes=[
             pltpu.VMEM((16, T), bf16),
             pltpu.VMEM((T, 16), bf16),
@@ -518,12 +562,16 @@
             pltpu.VMEM((40, 128), jnp.int32),
             pltpu.SMEM((40, 128), jnp.int32),
             pltpu.VMEM((256, 128), f32),
+            pltpu.VMEM((8, 8, 256), f32),
+            pltpu.VMEM((8, 8, 256), f32),
+            dma((2, 2)),
             pltpu.VMEM((16, 256, 256), bf16),
             pltpu.VMEM((8, 4, 256, 256), bf16),
             pltpu.VMEM((T, 256, 256), bf16),
             pltpu.VMEM((16, 256, 1), f32),
             pltpu.VMEM((32, 8, 256), f32),
             pltpu.VMEM((T, 256), f32),
+            pltpu.VMEM((256, T), f32),
             pltpu.VMEM((T, 256), f32),
             pltpu.VMEM((128, 256), f32),
             pltpu.VMEM((4, 16, 256), bf16),
@@ -551,10 +599,10 @@
 
 
 def shards(embeds, partners, counts):
-    args = embeds.reshape(4, 256, 256), partners, counts.reshape(1, 256)
+    args = embeds.reshape(4, 256, 256), partners.T, counts.reshape(1, 256)
     mapped, scale, most = transport(64, 0, *args)
     mapped, scale = lax.cond(
-        most[0, 0] <= 64.0,
+        most.reshape(()) <= 64.0,
         lambda mapped, scale, *args: (mapped, scale),
         lambda mapped, scale, *args: transport(128, 1, *args)[:2],
         mapped,

time: 106 us -> 91.8 us (0.87)
  Pallas kernels: 99.5 us -> 88.4 us
  local copies, waits for them, and re-layouts: 4.71 us -> 1.96 us
    pallas_call x1, Pallas kernels: 99.5 us -> 88.4 us  [transport(): pl.pallas_call(functools.partial(kernel, T), out_shape=(jax.ShapeDtypeStr...]
    unnamed x9 -> x8, local copies, waits for them, and re-layouts: 3.53 us -> 1.96 us
    slice x1 -> x0, local copies, waits for them, and re-layouts: 1.18 us -> none  [shards(): most[0, 0] <= 64.0]
where the time goes in v2:
time: 91.8 us; the launch traced here: 91.6 us
  Pallas kernels  88.4 us (96%)
  local copies, waits for them, and re-layouts  1.96 us (2%)
  between operations  1.24 us (1%)
    pallas_call x1, Pallas kernels, transport(): pl.pallas_call(functools.partial(kernel, T), out_shape=(jax.ShapeDtypeStr...  88.4 us
    unnamed x8, local copies, waits for them, and re-layouts  1.96 us

profile of v2, /device:TPU:1, one launch (start us, length us, event | category | flops | bytes accessed | tf_op | source)
XLA Modules:
  0.0 91.6 jit_solution(4707450706100087982)
XLA Ops:
  0.6 0.0 copy-start
  0.6 0.0 copy-start.1
  0.6 88.4 %transport_64.1 = (bf16[2,256,256]{2,1,0:T(8,128)(2,1)S(1)}, f32[4,256]{1,0:T(4,128)S(1)}, f32[1,1]{1,0:T(1,128)}) custom-call(bf16[4,256,256]{2,1,0:T(8,128)(2,1)} %bitcast.5, s32[32,256]{1,0:T(8,128)} %bitcast.8, s32[1,256]{1,0:T(1,128)} %bitcast.10), custom_call_target="tpu_custom_call" | custom-call | tf_op jit(solution)/shard_map/transport_64/pallas_call | solution.py:547
  89.7 0.0 copy-start.2
  89.7 0.0 copy-done
  89.7 0.0 copy-done.1
  89.7 0.7 copy-done.2
  90.3 0.7 copy.11
  91.0 0.6 copy.12
  (1 shorter events, 0.0 us)
Async XLA Ops:
  0.6 89.0 %copy-start = (bf16[1,4,256,256]{3,2,1,0:T(8,128)(2,1)S(1)}, bf16[1,4,256,256]{3,2,1,0:T(8,128)(2,1)}, u32[]{:S(2)}) copy-start(bf16[1,4,256,256]{3,2,1,0:T(8,128)(2,1)} %param.5) | copy-start | bytes 1572868
  0.6 89.0 %copy-start.1 = (s32[256,32]{0,1:T(8,128)S(1)}, s32[256,32]{0,1:T(8,128)}, u32[]{:S(2)}) copy-start(s32[256,32]{0,1:T(8,128)} %param.6) | copy-start | bytes 98308
  89.7 0.7 copy-start.2

commit v3 on v2

--- a/solution.py
+++ b/solution.py
@@ -42,12 +42,6 @@
 
 def dot_nt(a, b):
     return lax.dot_general(a, b, NT, preferred_element_type=f32)
-
-
-def split_dot(onehot, values):
-    high = values.astype(bf16)
-    low = (values - high.astype(f32)).astype(bf16)
-    return dot(onehot, high) + dot(onehot, low)
 
 
 def kernel(
@@ -63,6 +57,8 @@
     ob,
     obt,
     obd,
+    partners,
+    counts,
     index,
     idx,
     final,
@@ -82,6 +78,8 @@
     col_send,
     row_recv,
     col_recv,
+    scales,
+    half_swap,
     numer,
     ship,
     landed,
@@ -106,6 +104,8 @@
     greeted = [sibling]
     for m in range(1, 8):
         greeted += [member(at, flip_a, m, core), member(at, flip_b, m, core), member(at, flip_b, m, other)]
+        if m in (1, 2, 4):
+            greeted.append(member(at, flip_a, m, other))
     for peer in greeted:
         pl.semaphore_signal(barrier, inc=1, device_id=peer, device_id_type=MESH)
     pl.semaphore_wait(barrier, len(greeted))
@@ -121,71 +121,77 @@
             return abuf.at[pl.ds(slot * 2, 2), pl.ds(start, size)]
         return bbuf.at[slot, pl.ds(core * 2, 2), pl.ds(start, size)]
 
-    def unit_copy(cat, dim, piece, slot, src=None):
+    def send_unit(cat, dim, piece, slot):
         there = slot ^ (1 << dim)
-        return remote(
-            unit(cat, slot, piece) if src is None else src,
+        remote(
+            unit(cat, slot, piece),
             unit(cat, there, piece),
             out_sem.at[0],
             gather_sem.at[cat, piece, there],
             member(at, flips[cat], 1 << dim, core),
-        )
-
-    def send_unit(cat, dim, piece, slot):
-        copy = unit_copy(cat, dim, piece, slot)
-        copy.start()
-        return copy
-
-    def send_own(cat, src):
+        ).start()
+
+    def send_own(cat):
         for step in range(3):
             for dim in range(3):
                 piece = (dim - step) % 3
                 start, size = PIECES[piece]
-                unit_copy(cat, dim, piece, 0, None if src is None else src.at[:, pl.ds(start, size)]).start()
+                rows, there = pl.ds(start, size), 1 << dim
+                for half in range(2):
+                    two = pl.ds(half * 2, 2)
+                    remote(
+                        x_ref.at[two, rows],
+                        abuf.at[pl.ds(there * 2, 2), rows] if cat == 0 else bbuf.at[there, two, rows],
+                        out_sem.at[0],
+                        gather_sem.at[cat, piece, there],
+                        member(at, flips[cat], there, half),
+                    ).start()
 
     own_a_half, own_b = abuf.at[pl.ds(0, 2)], bbuf.at[0]
+
+    def landed_at(ref, sem):
+        pltpu.make_async_copy(ref, ref, sem).wait()
+
+    fetches = [
+        pltpu.make_async_copy(partners_ref, partners, own_sem.at[1]),
+        pltpu.make_async_copy(counts_ref, counts, own_sem.at[2]),
+    ]
 
     @pl.when(core == 0)
     def _():
         give = remote(x_ref.at[pl.ds(2, 2)], own_a_half, sib_sem.at[0], sib_sem.at[1], sibling)
         give.start()
-        send_own(0, x_ref.at[pl.ds(0, 2)])
         mine = pltpu.make_async_copy(x_ref.at[pl.ds(0, 2)], own_a_half, own_sem.at[0])
         mine.start()
+        send_own(0)
         mine.wait()
         give.wait_send()
-        pltpu.make_async_copy(own_b, own_b, sib_sem.at[1]).wait()
-        send_own(1, None)
+        landed_at(own_b, sib_sem.at[1])
 
     @pl.when(core == 1)
     def _():
         give = remote(x_ref, own_b, sib_sem.at[0], sib_sem.at[1], sibling)
         give.start()
-        send_own(1, x_ref.at[pl.ds(2, 2)])
         mine = pltpu.make_async_copy(x_ref, own_b, own_sem.at[0])
         mine.start()
+        send_own(1)
         mine.wait()
         give.wait_send()
-        pltpu.make_async_copy(own_a_half, own_a_half, sib_sem.at[1]).wait()
-        send_own(0, None)
-
-    sent = []
-    relays = []
+        landed_at(own_a_half, sib_sem.at[1])
+
+    for fetch in fetches:
+        fetch.start()
 
     def arrived(cat, piece, slot):
         here = unit(cat, slot, piece)
         pltpu.make_async_copy(here, here, gather_sem.at[cat, piece, slot]).wait()
         if cat == 1:
-            copy = remote(here, here, out_sem.at[1], relay_sem.at[slot], sibling)
-            copy.start()
-            relays.append(copy)
+            remote(here, here, out_sem.at[1], relay_sem.at[slot], sibling).start()
 
     def iota(shape, dim):
         return lax.broadcasted_iota(jnp.int32, shape, dim)
 
     diagonal = iota((128, 128), 0) == iota((128, 128), 1)
-
-    norm_copies = []
 
     def send_norms():
         def inverse_norm(block, scale):
@@ -202,19 +208,14 @@
             norm_bufs[1][0, i : i + 1] = inverse_norm(bbuf[0, i], 1.0 / 16.0)
         for cat in range(2):
             for m in range(1, 8):
-                copy = remote(
+                remote(
                     norm_bufs[cat].at[0], norm_bufs[cat].at[m], norm_sem.at[0, cat], norm_sem.at[1, cat],
                     member(at, flips[cat], m, core),
-                )
-                copy.start()
-                norm_copies.append(copy)
+                ).start()
 
     def take_norms():
         for cat in range(2):
-            got = norm_bufs[cat].at[pl.ds(1, 7)]
-            pltpu.make_async_copy(got, got, norm_sem.at[1, cat]).wait()
-        for copy in norm_copies:
-            copy.wait_send()
+            landed_at(norm_bufs[cat].at[pl.ds(1, 7)], norm_sem.at[1, cat])
         flipped_norms = jnp.transpose(
             jnp.concatenate([norm_bufs[0][m] for m in range(8)] + [jnp.zeros((64, 256), f32)], axis=0)
         )
@@ -234,8 +235,10 @@
         x, y, z = at
         own_low = [p % 2 for p in at]
         own_high = [p // 2 for p in at]
-        named_all = partners_ref[...]
-        limit_row = counts_ref[...]
+        for fetch in fetches:
+            fetch.wait()
+        named_all = partners[...]
+        limit_row = counts[...]
         r = iota((16, 256), 0)
         cx, cy, cz = [flipped([b], [p % 2]) + 2 * (p // 2) for b, p in zip(bits_of(r, (1, 2, 3)), at)]
         chosen = iota((16, 256), 1) == (cy * 16 + cx * 4 + cz) * 4 + 2 * core + (r & 1)
@@ -321,15 +324,15 @@
 
     send_norms()
     for cat, r, slot in received(lambda k0, k1, k2: k0):
-        sent.append(send_unit(cat, (r + 1) % 3, r, slot))
+        send_unit(cat, (r + 1) % 3, r, slot)
     for r in range(3):
         for cat in range(2):
-            sent.append(send_unit(cat, (r + 2) % 3, r, 1 << r))
+            send_unit(cat, (r + 2) % 3, r, 1 << r)
     for cat, r, slot in received(lambda k0, k1, k2: k1):
-        sent.append(send_unit(cat, (r + 2) % 3, r, slot))
+        send_unit(cat, (r + 2) % 3, r, slot)
     make_list()
     for cat, r, slot in received(lambda k0, k1, k2: k0 | k1):
-        sent.append(send_unit(cat, (r + 2) % 3, r, slot))
+        send_unit(cat, (r + 2) % 3, r, slot)
     for _ in received(lambda k0, k1, k2: k2):
         pass
     take_norms()
@@ -339,17 +342,8 @@
         pass
     for _ in received(lambda k0, k1, k2: 7):
         pass
-    for cat in range(2):
-        for step in range(3):
-            for dim in range(3):
-                sent.append(unit_copy(cat, dim, (dim - step) % 3, 0))
-    for copy in sent:
-        copy.wait_send()
-    for copy in relays:
-        copy.wait_send()
     for slot in range(1, 8):
-        here = bbuf.at[slot, pl.ds(other * 2, 2)]
-        pltpu.make_async_copy(here, here, relay_sem.at[slot]).wait()
+        landed_at(bbuf.at[slot, pl.ds(other * 2, 2)], relay_sem.at[slot])
 
     def build(i, c):
         for u in range(TURN):
@@ -387,10 +381,7 @@
 
         columns[...] = jnp.zeros((256, T), f32)
         lax.fori_loop(0, T // TURN, body, 0)
-        beside = columns[...]
-        high = beside.astype(bf16)
-        low = (beside - high.astype(f32)).astype(bf16)
-        return split_dot(oa[...], sums[...]) + dot_nt(oa[...], high) + dot_nt(oa[...], low)
+        return dot(oa[...], sums[...].astype(bf16)) + dot_nt(oa[...], columns[...].astype(bf16))
 
     def col_sweep():
         def body(i, c):
@@ -405,61 +396,56 @@
             return c
 
         lax.fori_loop(0, T // TURN, body, 0)
-        return split_dot(ob[...], sums[...])
+        return dot(ob[...], sums[...].astype(bf16))
 
     def row_exchange(phase, partial):
         row_send[phase] = partial.astype(bf16)
-        copies = []
         for m in range(1, 8):
-            copy = remote(
+            remote(
                 row_send.at[phase], row_recv.at[phase, m], row_sem.at[0, phase], row_sem.at[1, phase],
                 member(at, flip_a, m, core),
-            )
-            copy.start()
-            copies.append(copy)
-        return copies
-
-    def row_result(phase, copies):
-        got = row_recv.at[phase, pl.ds(1, 7)]
-        pltpu.make_async_copy(got, got, row_sem.at[1, phase]).wait()
+            ).start()
+
+    def row_result(phase):
+        landed_at(row_recv.at[phase, pl.ds(1, 7)], row_sem.at[1, phase])
         total = row_send[phase].astype(f32)
         for m in range(1, 8):
             total += row_recv[phase, m].astype(f32)
-        for copy in copies:
-            copy.wait_send()
         return total
 
     def col_exchange(phase, partial):
         col_send[phase] = partial.astype(bf16)
-        copies = []
-        for far in range(2):
+        for far, to in enumerate((core, other)):
             for m in range(8):
                 if far + m:
-                    copy = remote(
-                        col_send.at[phase], col_recv.at[phase, far * 8 + m], col_sem.at[0, phase],
-                        col_sem.at[1, phase], member(at, flip_b, m, other if far else core),
-                    )
-                    copy.start()
-                    copies.append(copy)
-        got = col_recv.at[phase, pl.ds(1, 15)]
-        pltpu.make_async_copy(got, got, col_sem.at[1, phase]).wait()
-        total = col_send[phase].astype(f32)
+                    remote(
+                        col_send.at[phase, pl.ds(pl.multiple_of(to * 16, 16), 16)],
+                        col_recv.at[phase, far * 8 + m],
+                        col_sem.at[0, phase],
+                        col_sem.at[1, phase],
+                        member(at, flip_b, m, to),
+                    ).start()
+        landed_at(col_recv.at[phase, pl.ds(1, 15)], col_sem.at[1, phase])
+        mine = pl.ds(pl.multiple_of(core * 16, 16), 16)
+        total = col_send[phase, mine].astype(f32)
         for m in range(1, 16):
             total += col_recv[phase, m].astype(f32)
-        for copy in copies:
-            copy.wait_send()
-        return total
+        scales[phase, mine] = 1.0 / (1.0 + total)
+        here = scales.at[phase, mine]
+        remote(here, here, half_swap.at[0, phase], half_swap.at[1, phase], sibling).start()
+        landed_at(scales.at[phase, pl.ds(pl.multiple_of(other * 16, 16), 16)], half_swap.at[1, phase])
+        return scales[phase]
 
     spread[...] = jnp.ones((T, 256), f32)
     for phase in range(ITERS):
-        scale_a = 1.0 / row_result(phase, row_exchange(phase, row_sweep()))
+        row_exchange(phase, row_sweep())
+        scale_a = 1.0 / row_result(phase)
         spread[...] = dot(oat[...], scale_a.astype(bf16))
-        scale_b = 1.0 / (1.0 + col_exchange(phase, col_sweep()))
+        scale_b = col_exchange(phase, col_sweep())
         spread[...] = dot(obt[...], scale_b.astype(bf16))
     x, y, z = at
     member_b = x // 2 + 2 * (y // 2) + 4 * (z // 2)
-    sums[pl.ds(0, 32), :] = scale_b
-    near_rows = sums[pl.ds(pl.multiple_of((member_b // 2) * 8, 8), 8), :]
+    near_rows = scales[ITERS - 1, pl.ds(pl.multiple_of((member_b // 2) * 8, 8), 8), :]
     scale_ref[...] = jnp.where(member_b % 2 == 0, near_rows[0:4], near_rows[4:8])
     dense[...] = dot(obd[...], scale_b.astype(bf16))
 
@@ -483,7 +469,6 @@
 
         lax.fori_loop(0, 2, body, 0)
 
-    halves = []
     final[...] = jnp.zeros((256, 128), f32)
 
     def send_half(piece, slot, dim, order):
@@ -491,12 +476,10 @@
         two, rows = pl.ds(slot * 2, 2), pl.ds(start, size)
         ship[two, rows, :] = numer[two, rows, :].astype(bf16)
         there = slot ^ (1 << dim)
-        copy = remote(
+        remote(
             ship.at[two, rows], landed.at[order, pl.ds(there * 2, 2), rows], out_sem.at[2], half_sem.at[order, piece, there],
             member(at, flip_a, 1 << dim, core),
-        )
-        copy.start()
-        halves.append(copy)
+        ).start()
 
     def add_half(piece, slot, order):
         start, size = PIECES[piece]
@@ -505,26 +488,29 @@
         pltpu.make_async_copy(here, here, half_sem.at[order, piece, slot]).wait()
         numer[two, rows, :] = numer[two, rows, :] + landed[order, two, rows, :].astype(f32)
 
-    for slot in (7, 3, 5, 6, 1, 2, 4, 0):
-        partial(slot)
-        for r in range(3):
-            if (slot >> r) & 1:
-                send_half(r, slot, r, 0)
-    for r in range(3):
-        k1, k2 = 1 << ((r + 1) % 3), 1 << ((r + 2) % 3)
+    def map_slots(slots):
+        for slot in slots:
+            partial(slot)
+            for r in range(3):
+                if (slot >> r) & 1:
+                    send_half(r, slot, r, 0)
+
+    near_dims = [(r, 1 << ((r + 1) % 3), 1 << ((r + 2) % 3)) for r in range(3)]
+    map_slots((7, 3, 5, 6))
+    for r, k1, k2 in near_dims:
         add_half(r, k1 | k2, 0)
         send_half(r, k1 | k2, (r + 1) % 3, 1)
-    row_copies = row_exchange(ITERS, jnp.transpose(final[...])[0:16])
-    for r in range(3):
-        k1, k2 = 1 << ((r + 1) % 3), 1 << ((r + 2) % 3)
+    map_slots((1, 2, 4))
+    for r, k1, k2 in near_dims:
         add_half(r, k1, 0)
         send_half(r, k1, (r + 1) % 3, 1)
-    for r in range(3):
-        k1, k2 = 1 << ((r + 1) % 3), 1 << ((r + 2) % 3)
+    map_slots((0,))
+    row_exchange(ITERS, jnp.transpose(final[...])[0:16])
+    for r, k1, k2 in near_dims:
         add_half(r, k2, 0)
         add_half(r, k2, 1)
         send_half(r, k2, (r + 2) % 3, 2)
-    sums[pl.ds(0, 16), :] = row_result(ITERS, row_copies)
+    sums[pl.ds(0, 16), :] = row_result(ITERS)
     own_a = x % 2 + 2 * (y % 2) + 4 * (z % 2)
     near_rows = sums[pl.ds(pl.multiple_of((own_a // 4) * 8, 8), 8), :]
     mine = near_rows[0:2]
@@ -537,8 +523,17 @@
     for i in range(2):
         inverse = column[:, i * 128 : i * 128 + 1]
         mapped_ref[i] = (numer[i] * inverse).astype(bf16)
-    for copy in halves:
-        copy.wait_send()
+    landed_at(abuf.at[pl.ds(2, 14)], out_sem.at[0])
+    landed_at(bbuf.at[pl.ds(1, 7), pl.ds(0, 2)], out_sem.at[0])
+    landed_at(bbuf.at[pl.ds(1, 7), pl.ds(0, 2)], out_sem.at[1])
+    landed_at(ship.at[pl.ds(2, 14)], out_sem.at[2])
+    for cat in range(2):
+        landed_at(norm_bufs[cat].at[pl.ds(1, 7)], norm_sem.at[0, cat])
+    for phase in range(ITERS + 1):
+        landed_at(row_recv.at[phase, pl.ds(1, 7)], row_sem.at[0, phase])
+    for phase in range(ITERS):
+        landed_at(col_recv.at[phase, pl.ds(1, 15)], col_sem.at[0, phase])
+        landed_at(scales.at[phase, pl.ds(0, 16)], half_swap.at[0, phase])
 
 
 def transport(T, cid, own, partners, counts):
@@ -551,7 +546,7 @@
             jax.ShapeDtypeStruct((4, 256), f32),
             jax.ShapeDtypeStruct((1, 1), f32),
         ),
-        in_specs=[pl.BlockSpec(memory_space=pl.ANY), vmem, vmem],
+        in_specs=[pl.BlockSpec(memory_space=pltpu.HBM)] * 3,
         out_specs=(vmem, vmem, pl.BlockSpec(memory_space=pltpu.SMEM)),
         scratch_shapes=[
             pltpu.VMEM((16, T), bf16),
@@ -559,6 +554,8 @@
             pltpu.VMEM((32, T), bf16),
             pltpu.VMEM((T, 32), bf16),
             pltpu.VMEM((128, 32), bf16),
+            pltpu.VMEM((32, 256), jnp.int32),
+            pltpu.VMEM((1, 256), jnp.int32),
             pltpu.VMEM((40, 128), jnp.int32),
             pltpu.SMEM((40, 128), jnp.int32),
             pltpu.VMEM((256, 128), f32),
@@ -577,11 +574,13 @@
             pltpu.VMEM((4, 16, 256), bf16),
             pltpu.VMEM((3, 32, 256), bf16),
             pltpu.VMEM((4, 8, 16, 256), bf16),
-            pltpu.VMEM((3, 16, 32, 256), bf16),
+            pltpu.VMEM((3, 16, 16, 256), bf16),
+            pltpu.VMEM((3, 32, 256), f32),
+            dma((2, 3)),
             pltpu.VMEM((16, 256, 256), f32),
             pltpu.VMEM((16, 256, 256), bf16),
             pltpu.VMEM((3, 16, 256, 256), bf16),
-            dma((1,)),
+            dma((3,)),
             dma((2,)),
             dma((2, 3, 8)),
             dma((8,)),

time: 91.8 us -> 90.9 us (level)
  no operation moved by 1% of the time
where the time goes in v3:
time: 90.9 us; the launch traced here: 90.7 us
  Pallas kernels  87.6 us (96%)
  local copies, waits for them, and re-layouts  1.96 us (2%)
  between operations  1.24 us (1%)
    pallas_call x1, Pallas kernels, transport(): pl.pallas_call(functools.partial(kernel, T), out_shape=(jax.ShapeDtypeStr...  87.6 us
    unnamed x8, local copies, waits for them, and re-layouts  1.96 us

profile of v3, /device:TPU:1, one launch (start us, length us, event | category | flops | bytes accessed | tf_op | source)
XLA Modules:
  0.0 90.7 jit_solution(17772229010527552935)
XLA Ops:
  0.6 0.0 copy-start
  0.6 0.0 copy-start.1
  0.6 87.6 %transport_64.1 = (bf16[2,256,256]{2,1,0:T(8,128)(2,1)S(1)}, f32[4,256]{1,0:T(4,128)S(1)}, f32[1,1]{1,0:T(1,128)}) custom-call(bf16[4,256,256]{2,1,0:T(8,128)(2,1)} %bitcast.5, s32[32,256]{1,0:T(8,128)} %bitcast.8, s32[1,256]{1,0:T(1,128)} %bitcast.10), custom_call_target="tpu_custom_call" | custom-call | tf_op jit(solution)/shard_map/transport_64/pallas_call | solution.py:542
  88.8 0.0 copy-start.2
  88.8 0.0 copy-done
  88.8 0.0 copy-done.1
  88.8 0.7 copy-done.2
  89.5 0.7 copy.11
  90.2 0.6 copy.12
  (1 shorter events, 0.0 us)
Async XLA Ops:
  0.6 88.2 %copy-start = (bf16[1,4,256,256]{3,2,1,0:T(8,128)(2,1)S(1)}, bf16[1,4,256,256]{3,2,1,0:T(8,128)(2,1)}, u32[]{:S(2)}) copy-start(bf16[1,4,256,256]{3,2,1,0:T(8,128)(2,1)} %param.5) | copy-start | bytes 1572868
  0.6 88.2 %copy-start.1 = (s32[256,32]{0,1:T(8,128)S(1)}, s32[256,32]{0,1:T(8,128)}, u32[]{:S(2)}) copy-start(s32[256,32]{0,1:T(8,128)} %param.6) | copy-start | bytes 98308
  88.8 0.7 copy-start.2

commit v4 on v3

--- a/solution.py
+++ b/solution.py
@@ -9,7 +9,8 @@
 from jax.sharding import PartitionSpec as P
 
 ITERS = 3
-TURN = 32
+TURN = 64
+FAR_FIRST = (7, 3, 5, 6, 1, 2, 4)
 GAIN = 20.0 * math.log2(math.e)
 MESH = pl.DeviceIdType.MESH
 NT = (((1,), (1,)), ((), ()))
@@ -52,6 +53,7 @@
     mapped_ref,
     scale_ref,
     most_ref,
+    counts_out,
     oa,
     oat,
     ob,
@@ -79,7 +81,6 @@
     row_recv,
     col_recv,
     scales,
-    half_swap,
     numer,
     ship,
     landed,
@@ -108,6 +109,12 @@
             greeted.append(member(at, flip_a, m, other))
     for peer in greeted:
         pl.semaphore_signal(barrier, inc=1, device_id=peer, device_id_type=MESH)
+    fetches = [
+        pltpu.make_async_copy(partners_ref, partners, own_sem.at[1]),
+        pltpu.make_async_copy(counts_ref, counts, own_sem.at[2]),
+    ]
+    for fetch in fetches:
+        fetch.start()
     pl.semaphore_wait(barrier, len(greeted))
 
     def remote(src, dst, send, recv, peer):
@@ -152,11 +159,6 @@
     def landed_at(ref, sem):
         pltpu.make_async_copy(ref, ref, sem).wait()
 
-    fetches = [
-        pltpu.make_async_copy(partners_ref, partners, own_sem.at[1]),
-        pltpu.make_async_copy(counts_ref, counts, own_sem.at[2]),
-    ]
-
     @pl.when(core == 0)
     def _():
         give = remote(x_ref.at[pl.ds(2, 2)], own_a_half, sib_sem.at[0], sib_sem.at[1], sibling)
@@ -179,8 +181,6 @@
         give.wait_send()
         landed_at(own_a_half, sib_sem.at[1])
 
-    for fetch in fetches:
-        fetch.start()
 
     def arrived(cat, piece, slot):
         here = unit(cat, slot, piece)
@@ -239,6 +239,7 @@
             fetch.wait()
         named_all = partners[...]
         limit_row = counts[...]
+        counts_out[...] = limit_row
         r = iota((16, 256), 0)
         cx, cy, cz = [flipped([b], [p % 2]) + 2 * (p // 2) for b, p in zip(bits_of(r, (1, 2, 3)), at)]
         chosen = iota((16, 256), 1) == (cy * 16 + cx * 4 + cz) * 4 + 2 * core + (r & 1)
@@ -322,6 +323,7 @@
                 arrived(cat, r, slot)
                 yield cat, r, slot
 
+    make_list()
     send_norms()
     for cat, r, slot in received(lambda k0, k1, k2: k0):
         send_unit(cat, (r + 1) % 3, r, slot)
@@ -330,7 +332,6 @@
             send_unit(cat, (r + 2) % 3, r, 1 << r)
     for cat, r, slot in received(lambda k0, k1, k2: k1):
         send_unit(cat, (r + 2) % 3, r, slot)
-    make_list()
     for cat, r, slot in received(lambda k0, k1, k2: k0 | k1):
         send_unit(cat, (r + 2) % 3, r, slot)
     for _ in received(lambda k0, k1, k2: k2):
@@ -400,7 +401,7 @@
 
     def row_exchange(phase, partial):
         row_send[phase] = partial.astype(bf16)
-        for m in range(1, 8):
+        for m in FAR_FIRST:
             remote(
                 row_send.at[phase], row_recv.at[phase, m], row_sem.at[0, phase], row_sem.at[1, phase],
                 member(at, flip_a, m, core),
@@ -415,26 +416,18 @@
 
     def col_exchange(phase, partial):
         col_send[phase] = partial.astype(bf16)
-        for far, to in enumerate((core, other)):
-            for m in range(8):
+        for m in FAR_FIRST + (0,):
+            for far, to in ((1, other), (0, core)):
                 if far + m:
                     remote(
-                        col_send.at[phase, pl.ds(pl.multiple_of(to * 16, 16), 16)],
-                        col_recv.at[phase, far * 8 + m],
-                        col_sem.at[0, phase],
-                        col_sem.at[1, phase],
-                        member(at, flip_b, m, to),
+                        col_send.at[phase], col_recv.at[phase, far * 8 + m], col_sem.at[0, phase],
+                        col_sem.at[1, phase], member(at, flip_b, m, to),
                     ).start()
         landed_at(col_recv.at[phase, pl.ds(1, 15)], col_sem.at[1, phase])
-        mine = pl.ds(pl.multiple_of(core * 16, 16), 16)
-        total = col_send[phase, mine].astype(f32)
+        total = col_send[phase].astype(f32)
         for m in range(1, 16):
             total += col_recv[phase, m].astype(f32)
-        scales[phase, mine] = 1.0 / (1.0 + total)
-        here = scales.at[phase, mine]
-        remote(here, here, half_swap.at[0, phase], half_swap.at[1, phase], sibling).start()
-        landed_at(scales.at[phase, pl.ds(pl.multiple_of(other * 16, 16), 16)], half_swap.at[1, phase])
-        return scales[phase]
+        return 1.0 / (1.0 + total)
 
     spread[...] = jnp.ones((T, 256), f32)
     for phase in range(ITERS):
@@ -445,7 +438,8 @@
         spread[...] = dot(obt[...], scale_b.astype(bf16))
     x, y, z = at
     member_b = x // 2 + 2 * (y // 2) + 4 * (z // 2)
-    near_rows = scales[ITERS - 1, pl.ds(pl.multiple_of((member_b // 2) * 8, 8), 8), :]
+    scales[...] = scale_b
+    near_rows = scales[pl.ds(pl.multiple_of((member_b // 2) * 8, 8), 8), :]
     scale_ref[...] = jnp.where(member_b % 2 == 0, near_rows[0:4], near_rows[4:8])
     dense[...] = dot(obd[...], scale_b.astype(bf16))
 
@@ -533,7 +527,6 @@
         landed_at(row_recv.at[phase, pl.ds(1, 7)], row_sem.at[0, phase])
     for phase in range(ITERS):
         landed_at(col_recv.at[phase, pl.ds(1, 15)], col_sem.at[0, phase])
-        landed_at(scales.at[phase, pl.ds(0, 16)], half_swap.at[0, phase])
 
 
 def transport(T, cid, own, partners, counts):
@@ -545,9 +538,10 @@
             jax.ShapeDtypeStruct((2, 256, 256), bf16),
             jax.ShapeDtypeStruct((4, 256), f32),
             jax.ShapeDtypeStruct((1, 1), f32),
+            jax.ShapeDtypeStruct((1, 256), jnp.int32),
         ),
         in_specs=[pl.BlockSpec(memory_space=pltpu.HBM)] * 3,
-        out_specs=(vmem, vmem, pl.BlockSpec(memory_space=pltpu.SMEM)),
+        out_specs=(vmem, vmem, pl.BlockSpec(memory_space=pltpu.SMEM), vmem),
         scratch_shapes=[
             pltpu.VMEM((16, T), bf16),
             pltpu.VMEM((T, 16), bf16),
@@ -574,9 +568,8 @@
             pltpu.VMEM((4, 16, 256), bf16),
             pltpu.VMEM((3, 32, 256), bf16),
             pltpu.VMEM((4, 8, 16, 256), bf16),
-            pltpu.VMEM((3, 16, 16, 256), bf16),
-            pltpu.VMEM((3, 32, 256), f32),
-            dma((2, 3)),
+            pltpu.VMEM((3, 16, 32, 256), bf16),
+            pltpu.VMEM((32, 256), f32),
             pltpu.VMEM((16, 256, 256), f32),
             pltpu.VMEM((16, 256, 256), bf16),
             pltpu.VMEM((3, 16, 256, 256), bf16),
@@ -599,14 +592,15 @@
 
 def shards(embeds, partners, counts):
     args = embeds.reshape(4, 256, 256), partners.T, counts.reshape(1, 256)
-    mapped, scale, most = transport(64, 0, *args)
+    mapped, scale, most, limits = transport(64, 0, *args)
     mapped, scale = lax.cond(
         most.reshape(()) <= 64.0,
         lambda mapped, scale, *args: (mapped, scale),
         lambda mapped, scale, *args: transport(128, 1, *args)[:2],
         mapped,
         scale,
-        *args,
+        *args[:2],
+        limits,
     )
     return mapped.reshape(1, 1, 2, 256, 256), scale
 

time: 90.9 us -> 87.2 us (0.959)
  Pallas kernels: 87.6 us -> 84.1 us
    pallas_call x1, Pallas kernels: 87.6 us -> 84.1 us  [transport(): pl.pallas_call(functools.partial(kernel, T), out_shape=(jax.ShapeDtypeStr...]
    unnamed x8 -> x6, local copies, waits for them, and re-layouts: 1.96 us -> 1.31 us
where the time goes in v4:
time: 87.2 us; the launch traced here: 87 us
  Pallas kernels  84.1 us (96%)
  between operations  1.37 us (2%)
  local copies, waits for them, and re-layouts  1.31 us (2%)
    pallas_call x1, Pallas kernels, transport(): pl.pallas_call(functools.partial(kernel, T), out_shape=(jax.ShapeDtypeStr...  84.1 us

profile of v4, /device:TPU:1, one launch (start us, length us, event | category | flops | bytes accessed | tf_op | source)
XLA Modules:
  0.0 87.0 jit_solution(14922261994372802876)
XLA Ops:
  0.6 0.0 copy-start
  0.6 0.0 copy-start.1
  0.6 84.1 %transport_64.1 = (bf16[2,256,256]{2,1,0:T(8,128)(2,1)S(1)}, f32[4,256]{1,0:T(4,128)S(1)}, f32[1,1]{1,0:T(1,128)}, s32[1,256]{1,0:T(1,128)S(1)}) custom-call(bf16[4,256,256]{2,1,0:T(8,128)(2,1)} %bitcast.5, s32[32,256]{1,0:T(8,128)} %bitcast.8, s32[1,256]{1,0:T(1,128)} %bitcast.10), custom_call_target="tpu_custom_call" | custom-call | tf_op jit(solution)/shard_map/transport_64/pallas_call | solution.py:535
  85.4 0.0 copy-done
  85.4 0.0 copy-done.1
  85.4 0.3 conditional.1
  85.7 0.7 copy.11
  86.4 0.6 copy.12
Async XLA Ops:
  0.6 84.8 %copy-start = (bf16[1,4,256,256]{3,2,1,0:T(8,128)(2,1)S(1)}, bf16[1,4,256,256]{3,2,1,0:T(8,128)(2,1)}, u32[]{:S(2)}) copy-start(bf16[1,4,256,256]{3,2,1,0:T(8,128)(2,1)} %param.5) | copy-start | bytes 1572868
  0.6 84.8 %copy-start.1 = (s32[256,32]{0,1:T(8,128)S(1)}, s32[256,32]{0,1:T(8,128)}, u32[]{:S(2)}) copy-start(s32[256,32]{0,1:T(8,128)} %param.6) | copy-start | bytes 98308

commit v5 on v4

--- a/solution.py
+++ b/solution.py
@@ -93,6 +93,7 @@
     col_sem,
     half_sem,
     index_sem,
+    ready,
 ):
     core, at = place()
     other = 1 - core
@@ -102,11 +103,10 @@
     bufs = (abuf, bbuf)
 
     barrier = pltpu.get_barrier_semaphore()
-    greeted = [sibling]
-    for m in range(1, 8):
-        greeted += [member(at, flip_a, m, core), member(at, flip_b, m, core), member(at, flip_b, m, other)]
-        if m in (1, 2, 4):
-            greeted.append(member(at, flip_a, m, other))
+    greeted = []
+    for m in (1, 2, 4):
+        greeted += [member(at, flip, m, to) for flip in (flip_a, flip_b) for to in (other, core)]
+    greeted.append(sibling)
     for peer in greeted:
         pl.semaphore_signal(barrier, inc=1, device_id=peer, device_id_type=MESH)
     fetches = [
@@ -116,6 +116,13 @@
     for fetch in fetches:
         fetch.start()
     pl.semaphore_wait(barrier, len(greeted))
+
+    def greet(level):
+        for peer in greeted:
+            pl.semaphore_signal(ready.at[level], inc=1, device_id=peer, device_id_type=MESH)
+
+    def greeted_by_all(level):
+        pl.semaphore_wait(ready.at[level], len(greeted))
 
     def remote(src, dst, send, recv, peer):
         return pltpu.make_async_remote_copy(
@@ -166,6 +173,7 @@
         mine = pltpu.make_async_copy(x_ref.at[pl.ds(0, 2)], own_a_half, own_sem.at[0])
         mine.start()
         send_own(0)
+        greet(0)
         mine.wait()
         give.wait_send()
         landed_at(own_b, sib_sem.at[1])
@@ -177,6 +185,7 @@
         mine = pltpu.make_async_copy(x_ref, own_b, own_sem.at[0])
         mine.start()
         send_own(1)
+        greet(0)
         mine.wait()
         give.wait_send()
         landed_at(own_a_half, sib_sem.at[1])
@@ -193,7 +202,7 @@
 
     diagonal = iota((128, 128), 0) == iota((128, 128), 1)
 
-    def send_norms():
+    def own_norms():
         def inverse_norm(block, scale):
             halves = []
             for h in range(2):
@@ -206,6 +215,8 @@
             norm_bufs[0][0, i : i + 1] = inverse_norm(abuf[i], GAIN / 16.0)
         for i in range(4):
             norm_bufs[1][0, i : i + 1] = inverse_norm(bbuf[0, i], 1.0 / 16.0)
+
+    def share_norms():
         for cat in range(2):
             for m in range(1, 8):
                 remote(
@@ -324,25 +335,26 @@
                 yield cat, r, slot
 
     make_list()
-    send_norms()
+    greeted_by_all(0)
+    greet(1)
+    own_norms()
     for cat, r, slot in received(lambda k0, k1, k2: k0):
         send_unit(cat, (r + 1) % 3, r, slot)
     for r in range(3):
         for cat in range(2):
             send_unit(cat, (r + 2) % 3, r, 1 << r)
+    greeted_by_all(1)
+    share_norms()
     for cat, r, slot in received(lambda k0, k1, k2: k1):
         send_unit(cat, (r + 2) % 3, r, slot)
     for cat, r, slot in received(lambda k0, k1, k2: k0 | k1):
         send_unit(cat, (r + 2) % 3, r, slot)
-    for _ in received(lambda k0, k1, k2: k2):
-        pass
+    for cat in (1, 0):
+        for rest in (0, 1, 2, 3):
+            for r in range(3):
+                near, far = (rest & 1) << r, (rest >> 1) << ((r + 1) % 3)
+                arrived(cat, r, near | far | (1 << ((r + 2) % 3)))
     take_norms()
-    for _ in received(lambda k0, k1, k2: k2 | k0):
-        pass
-    for _ in received(lambda k0, k1, k2: k2 | k1):
-        pass
-    for _ in received(lambda k0, k1, k2: 7):
-        pass
     for slot in range(1, 8):
         landed_at(bbuf.at[slot, pl.ds(other * 2, 2)], relay_sem.at[slot])
 
@@ -455,7 +467,10 @@
                 half = weights[:, 0:128] + weights[:, 128:256]
                 total = part if total is None else total + part
                 mass = half if mass is None else mass + half
-            numer[a] = total
+            if slot != 7:
+                numer[a] = total
+            if slot:
+                ship[a] = total.astype(bf16)
             column = jnp.sum(mass, axis=1, keepdims=True)
             a_at = flipped([(slot >> k) & 1 for k in range(3)], [p % 2 for p in at]) * 2 + i
             final[...] = jnp.where(iota((256, 128), 1) == a_at, column, final[...])
@@ -468,7 +483,8 @@
     def send_half(piece, slot, dim, order):
         start, size = PIECES[piece]
         two, rows = pl.ds(slot * 2, 2), pl.ds(start, size)
-        ship[two, rows, :] = numer[two, rows, :].astype(bf16)
+        if order:
+            ship[two, rows, :] = numer[two, rows, :].astype(bf16)
         there = slot ^ (1 << dim)
         remote(
             ship.at[two, rows], landed.at[order, pl.ds(there * 2, 2), rows], out_sem.at[2], half_sem.at[order, piece, there],
@@ -500,10 +516,23 @@
         send_half(r, k1, (r + 1) % 3, 1)
     map_slots((0,))
     row_exchange(ITERS, jnp.transpose(final[...])[0:16])
+
+    landed_at(abuf.at[pl.ds(2, 14)], out_sem.at[0])
+    landed_at(bbuf.at[pl.ds(1, 7), pl.ds(0, 2)], out_sem.at[0])
+    landed_at(bbuf.at[pl.ds(1, 7), pl.ds(0, 2)], out_sem.at[1])
+    for cat in range(2):
+        landed_at(norm_bufs[cat].at[pl.ds(1, 7)], norm_sem.at[0, cat])
+    for phase in range(ITERS):
+        landed_at(row_recv.at[phase, pl.ds(1, 7)], row_sem.at[0, phase])
+        landed_at(col_recv.at[phase, pl.ds(1, 15)], col_sem.at[0, phase])
+
     for r, k1, k2 in near_dims:
         add_half(r, k2, 0)
         add_half(r, k2, 1)
         send_half(r, k2, (r + 2) % 3, 2)
+    for r in range(3):
+        add_half(r, 0, 0)
+        add_half(r, 0, 1)
     sums[pl.ds(0, 16), :] = row_result(ITERS)
     own_a = x % 2 + 2 * (y % 2) + 4 * (z % 2)
     near_rows = sums[pl.ds(pl.multiple_of((own_a // 4) * 8, 8), 8), :]
@@ -512,21 +541,14 @@
         mine = jnp.where(own_a % 4 == k, near_rows[2 * k : 2 * k + 2], mine)
     column = jnp.transpose(jnp.broadcast_to(1.0 / mine[:, None, :], (2, 128, 256)).reshape(256, 256))
     for r in range(3):
-        for order in range(3):
-            add_half(r, 0, order)
-    for i in range(2):
-        inverse = column[:, i * 128 : i * 128 + 1]
-        mapped_ref[i] = (numer[i] * inverse).astype(bf16)
-    landed_at(abuf.at[pl.ds(2, 14)], out_sem.at[0])
-    landed_at(bbuf.at[pl.ds(1, 7), pl.ds(0, 2)], out_sem.at[0])
-    landed_at(bbuf.at[pl.ds(1, 7), pl.ds(0, 2)], out_sem.at[1])
+        start, size = PIECES[r]
+        rows = pl.ds(start, size)
+        landed_at(landed.at[2, pl.ds(0, 2), rows], half_sem.at[2, r, 0])
+        for i in range(2):
+            inverse = column[start : start + size, i * 128 : i * 128 + 1]
+            mapped_ref[i, rows, :] = ((numer[i, rows, :] + landed[2, i, rows, :].astype(f32)) * inverse).astype(bf16)
     landed_at(ship.at[pl.ds(2, 14)], out_sem.at[2])
-    for cat in range(2):
-        landed_at(norm_bufs[cat].at[pl.ds(1, 7)], norm_sem.at[0, cat])
-    for phase in range(ITERS + 1):
-        landed_at(row_recv.at[phase, pl.ds(1, 7)], row_sem.at[0, phase])
-    for phase in range(ITERS):
-        landed_at(col_recv.at[phase, pl.ds(1, 15)], col_sem.at[0, phase])
+    landed_at(row_recv.at[ITERS, pl.ds(1, 7)], row_sem.at[0, ITERS])
 
 
 def transport(T, cid, own, partners, counts):
@@ -582,6 +604,7 @@
             dma((2, 3)),
             dma((3, 3, 8)),
             dma((1,)),
+            pltpu.SemaphoreType.REGULAR((2,)),
         ],
         compiler_params=pltpu.CompilerParams(
             collective_id=cid, has_side_effects=True, vmem_limit_bytes=60 << 20

time: 87.2 us -> 85.2 us (0.977)
  Pallas kernels: 84.1 us -> 82 us
    pallas_call x1, Pallas kernels: 84.1 us -> 82 us  [transport(): pl.pallas_call(functools.partial(kernel, T), out_shape=(jax.ShapeDtypeStr...]
where the time goes in v5:
time: 85.2 us; the launch traced here: 85 us
  Pallas kernels  82 us (96%)
  between operations  1.37 us (2%)
  local copies, waits for them, and re-layouts  1.31 us (2%)
    pallas_call x1, Pallas kernels, transport(): pl.pallas_call(functools.partial(kernel, T), out_shape=(jax.ShapeDtypeStr...  82 us

profile of v5, /device:TPU:1, one launch (start us, length us, event | category | flops | bytes accessed | tf_op | source)
XLA Modules:
  0.0 85.0 jit_solution(6415757180939667365)
XLA Ops:
  0.6 0.0 copy-start
  0.6 0.0 copy-start.1
  0.6 82.0 %transport_64.1 = (bf16[2,256,256]{2,1,0:T(8,128)(2,1)S(1)}, f32[4,256]{1,0:T(4,128)S(1)}, f32[1,1]{1,0:T(1,128)}, s32[1,256]{1,0:T(1,128)S(1)}) custom-call(bf16[4,256,256]{2,1,0:T(8,128)(2,1)} %bitcast.5, s32[32,256]{1,0:T(8,128)} %bitcast.8, s32[1,256]{1,0:T(1,128)} %bitcast.10), custom_call_target="tpu_custom_call" | custom-call | tf_op jit(solution)/shard_map/transport_64/pallas_call | solution.py:557
  83.4 0.0 copy-done
  83.4 0.0 copy-done.1
  83.4 0.3 conditional.1
  83.7 0.7 copy.11
  84.4 0.6 copy.12
Async XLA Ops:
  0.6 82.8 %copy-start = (bf16[1,4,256,256]{3,2,1,0:T(8,128)(2,1)S(1)}, bf16[1,4,256,256]{3,2,1,0:T(8,128)(2,1)}, u32[]{:S(2)}) copy-start(bf16[1,4,256,256]{3,2,1,0:T(8,128)(2,1)} %param.5) | copy-start | bytes 1572868
  0.6 82.8 %copy-start.1 = (s32[256,32]{0,1:T(8,128)S(1)}, s32[256,32]{0,1:T(8,128)}, u32[]{:S(2)}) copy-start(s32[256,32]{0,1:T(8,128)} %param.6) | copy-start | bytes 98308

commit v6 on v5

--- a/solution.py
+++ b/solution.py
@@ -16,7 +16,11 @@
 NT = (((1,), (1,)), ((), ()))
 f32 = jnp.float32
 bf16 = jnp.bfloat16
-PIECES = ((0, 96), (96, 80), (176, 80))
+PIECES = (((0, 96), (0, 80)), ((96, 80), (80, 96)), ((176, 80), (176, 80)))
+
+
+def total_rows(piece):
+    return sum(size for _, size in PIECES[piece])
 
 
 def place():
@@ -130,36 +134,33 @@
         )
 
     def unit(cat, slot, piece):
-        start, size = PIECES[piece]
+        rows = [pl.ds(start, size) for start, size in PIECES[piece]]
         if cat == 0:
-            return abuf.at[pl.ds(slot * 2, 2), pl.ds(start, size)]
-        return bbuf.at[slot, pl.ds(core * 2, 2), pl.ds(start, size)]
+            return [abuf.at[slot * 2 + i, rows[i]] for i in range(2)]
+        return [bbuf.at[slot, core * 2 + i, rows[i]] for i in range(2)]
 
     def send_unit(cat, dim, piece, slot):
         there = slot ^ (1 << dim)
-        remote(
-            unit(cat, slot, piece),
-            unit(cat, there, piece),
-            out_sem.at[0],
-            gather_sem.at[cat, piece, there],
-            member(at, flips[cat], 1 << dim, core),
-        ).start()
+        for src, dst in zip(unit(cat, slot, piece), unit(cat, there, piece)):
+            remote(
+                src, dst, out_sem.at[0], gather_sem.at[cat, piece, there], member(at, flips[cat], 1 << dim, core)
+            ).start()
 
     def send_own(cat):
         for step in range(3):
             for dim in range(3):
                 piece = (dim - step) % 3
-                start, size = PIECES[piece]
-                rows, there = pl.ds(start, size), 1 << dim
+                there = 1 << dim
                 for half in range(2):
-                    two = pl.ds(half * 2, 2)
-                    remote(
-                        x_ref.at[two, rows],
-                        abuf.at[pl.ds(there * 2, 2), rows] if cat == 0 else bbuf.at[there, two, rows],
-                        out_sem.at[0],
-                        gather_sem.at[cat, piece, there],
-                        member(at, flips[cat], there, half),
-                    ).start()
+                    for i, (start, size) in enumerate(PIECES[piece]):
+                        rows = pl.ds(start, size)
+                        remote(
+                            x_ref.at[half * 2 + i, rows],
+                            abuf.at[there * 2 + i, rows] if cat == 0 else bbuf.at[there, half * 2 + i, rows],
+                            out_sem.at[0],
+                            gather_sem.at[cat, piece, there],
+                            member(at, flips[cat], there, half),
+                        ).start()
 
     own_a_half, own_b = abuf.at[pl.ds(0, 2)], bbuf.at[0]
 
@@ -192,10 +193,13 @@
 
 
     def arrived(cat, piece, slot):
-        here = unit(cat, slot, piece)
-        pltpu.make_async_copy(here, here, gather_sem.at[cat, piece, slot]).wait()
+        rows = pl.ds(0, total_rows(piece))
+        landed_at(
+            abuf.at[slot * 2, rows] if cat == 0 else bbuf.at[slot, core * 2, rows], gather_sem.at[cat, piece, slot]
+        )
         if cat == 1:
-            remote(here, here, out_sem.at[1], relay_sem.at[slot], sibling).start()
+            for here in unit(cat, slot, piece):
+                remote(here, here, out_sem.at[1], relay_sem.at[slot], sibling).start()
 
     def iota(shape, dim):
         return lax.broadcasted_iota(jnp.int32, shape, dim)
@@ -481,22 +485,27 @@
     final[...] = jnp.zeros((256, 128), f32)
 
     def send_half(piece, slot, dim, order):
-        start, size = PIECES[piece]
-        two, rows = pl.ds(slot * 2, 2), pl.ds(start, size)
-        if order:
-            ship[two, rows, :] = numer[two, rows, :].astype(bf16)
         there = slot ^ (1 << dim)
-        remote(
-            ship.at[two, rows], landed.at[order, pl.ds(there * 2, 2), rows], out_sem.at[2], half_sem.at[order, piece, there],
-            member(at, flip_a, 1 << dim, core),
-        ).start()
+        for i, (start, size) in enumerate(PIECES[piece]):
+            rows = pl.ds(start, size)
+            if order:
+                ship[slot * 2 + i, rows, :] = numer[slot * 2 + i, rows, :].astype(bf16)
+            remote(
+                ship.at[slot * 2 + i, rows],
+                landed.at[order, there * 2 + i, rows],
+                out_sem.at[2],
+                half_sem.at[order, piece, there],
+                member(at, flip_a, 1 << dim, core),
+            ).start()
+
+    def half_landed(piece, slot, order):
+        landed_at(landed.at[order, slot * 2, pl.ds(0, total_rows(piece))], half_sem.at[order, piece, slot])
 
     def add_half(piece, slot, order):
-        start, size = PIECES[piece]
-        two, rows = pl.ds(slot * 2, 2), pl.ds(start, size)
-        here = landed.at[order, two, rows]
-        pltpu.make_async_copy(here, here, half_sem.at[order, piece, slot]).wait()
-        numer[two, rows, :] = numer[two, rows, :] + landed[order, two, rows, :].astype(f32)
+        half_landed(piece, slot, order)
+        for i, (start, size) in enumerate(PIECES[piece]):
+            a, rows = slot * 2 + i, pl.ds(start, size)
+            numer[a, rows, :] = numer[a, rows, :] + landed[order, a, rows, :].astype(f32)
 
     def map_slots(slots):
         for slot in slots:
@@ -541,10 +550,9 @@
         mine = jnp.where(own_a % 4 == k, near_rows[2 * k : 2 * k + 2], mine)
     column = jnp.transpose(jnp.broadcast_to(1.0 / mine[:, None, :], (2, 128, 256)).reshape(256, 256))
     for r in range(3):
-        start, size = PIECES[r]
-        rows = pl.ds(start, size)
-        landed_at(landed.at[2, pl.ds(0, 2), rows], half_sem.at[2, r, 0])
-        for i in range(2):
+        half_landed(r, 0, 2)
+        for i, (start, size) in enumerate(PIECES[r]):
+            rows = pl.ds(start, size)
             inverse = column[start : start + size, i * 128 : i * 128 + 1]
             mapped_ref[i, rows, :] = ((numer[i, rows, :] + landed[2, i, rows, :].astype(f32)) * inverse).astype(bf16)
     landed_at(ship.at[pl.ds(2, 14)], out_sem.at[2])

time: 85.2 us -> 84.9 us (level)
  no operation moved by 1% of the time
where the time goes in v6:
time: 84.9 us; the launch traced here: 84.8 us
  Pallas kernels  81.8 us (96%)
  between operations  1.37 us (2%)
  local copies, waits for them, and re-layouts  1.31 us (2%)
    pallas_call x1, Pallas kernels, transport(): pl.pallas_call(functools.partial(kernel, T), out_shape=(jax.ShapeDtypeStr...  81.8 us

profile of v6, /device:TPU:1, one launch (start us, length us, event | category | flops | bytes accessed | tf_op | source)
XLA Modules:
  0.0 84.8 jit_solution(11868101696922066845)
XLA Ops:
  0.6 0.0 copy-start
  0.6 0.0 copy-start.1
  0.6 81.8 %transport_64.1 = (bf16[2,256,256]{2,1,0:T(8,128)(2,1)S(1)}, f32[4,256]{1,0:T(4,128)S(1)}, f32[1,1]{1,0:T(1,128)}, s32[1,256]{1,0:T(1,128)S(1)}) custom-call(bf16[4,256,256]{2,1,0:T(8,128)(2,1)} %bitcast.5, s32[32,256]{1,0:T(8,128)} %bitcast.8, s32[1,256]{1,0:T(1,128)} %bitcast.10), custom_call_target="tpu_custom_call" | custom-call | tf_op jit(solution)/shard_map/transport_64/pallas_call | solution.py:565
  83.2 0.0 copy-done
  83.2 0.0 copy-done.1
  83.2 0.3 conditional.1
  83.5 0.7 copy.11
  84.2 0.6 copy.12
Async XLA Ops:
  0.6 82.6 %copy-start = (bf16[1,4,256,256]{3,2,1,0:T(8,128)(2,1)S(1)}, bf16[1,4,256,256]{3,2,1,0:T(8,128)(2,1)}, u32[]{:S(2)}) copy-start(bf16[1,4,256,256]{3,2,1,0:T(8,128)(2,1)} %param.5) | copy-start | bytes 1572868
  0.6 82.6 %copy-start.1 = (s32[256,32]{0,1:T(8,128)S(1)}, s32[256,32]{0,1:T(8,128)}, u32[]{:S(2)}) copy-start(s32[256,32]{0,1:T(8,128)} %param.6) | copy-start | bytes 98308

commit v7 on v6

--- a/solution.py
+++ b/solution.py
@@ -432,13 +432,16 @@
 
     def col_exchange(phase, partial):
         col_send[phase] = partial.astype(bf16)
-        for m in FAR_FIRST + (0,):
-            for far, to in ((1, other), (0, core)):
-                if far + m:
-                    remote(
-                        col_send.at[phase], col_recv.at[phase, far * 8 + m], col_sem.at[0, phase],
-                        col_sem.at[1, phase], member(at, flip_b, m, to),
-                    ).start()
+        def give(far, m, to):
+            remote(
+                col_send.at[phase], col_recv.at[phase, far * 8 + m], col_sem.at[0, phase],
+                col_sem.at[1, phase], member(at, flip_b, m, to),
+            ).start()
+
+        for m in FAR_FIRST:
+            give(core, m, 0)
+            give(other, m, 1)
+        give(1, 0, other)
         landed_at(col_recv.at[phase, pl.ds(1, 15)], col_sem.at[1, phase])
         total = col_send[phase].astype(f32)
         for m in range(1, 16):

time: 84.9 us -> 85 us (level)
  no operation moved by 1% of the time
where the time goes in v7:
time: 85 us; the launch traced here: 84.9 us
  Pallas kernels  81.9 us (96%)
  between operations  1.37 us (2%)
  local copies, waits for them, and re-layouts  1.31 us (2%)
    pallas_call x1, Pallas kernels, transport(): pl.pallas_call(functools.partial(kernel, T), out_shape=(jax.ShapeDtypeStr...  81.9 us

profile of v7, /device:TPU:1, one launch (start us, length us, event | category | flops | bytes accessed | tf_op | source)
XLA Modules:
  0.0 84.9 jit_solution(2478071792858082192)
XLA Ops:
  0.6 0.0 copy-start
  0.6 0.0 copy-start.1
  0.6 81.9 %transport_64.1 = (bf16[2,256,256]{2,1,0:T(8,128)(2,1)S(1)}, f32[4,256]{1,0:T(4,128)S(1)}, f32[1,1]{1,0:T(1,128)}, s32[1,256]{1,0:T(1,128)S(1)}) custom-call(bf16[4,256,256]{2,1,0:T(8,128)(2,1)} %bitcast.5, s32[32,256]{1,0:T(8,128)} %bitcast.8, s32[1,256]{1,0:T(1,128)} %bitcast.10), custom_call_target="tpu_custom_call" | custom-call | tf_op jit(solution)/shard_map/transport_64/pallas_call | solution.py:568
  83.3 0.0 copy-done
  83.3 0.0 copy-done.1
  83.3 0.3 conditional.1
  83.6 0.7 copy.11
  84.3 0.6 copy.12
Async XLA Ops:
  0.6 82.6 %copy-start = (bf16[1,4,256,256]{3,2,1,0:T(8,128)(2,1)S(1)}, bf16[1,4,256,256]{3,2,1,0:T(8,128)(2,1)}, u32[]{:S(2)}) copy-start(bf16[1,4,256,256]{3,2,1,0:T(8,128)(2,1)} %param.5) | copy-start | bytes 1572868
  0.6 82.6 %copy-start.1 = (s32[256,32]{0,1:T(8,128)S(1)}, s32[256,32]{0,1:T(8,128)}, u32[]{:S(2)}) copy-start(s32[256,32]{0,1:T(8,128)} %param.6) | copy-start | bytes 98308
